TPU v7x, 256 devices: a whole 4x4x8 slice. The times are simulated.
256 devices in a mesh: chan: 64 (over z, y, core), row: 4 (over x).
Axes of the slice: x: 4, y: 4, z: 8, core: 2. Of those that a mesh axis runs over, the one named last changes fastest.
Arguments:
- generator: float32 [64, 1280, 1280], P('chan', 'row'), as said below
- hamiltonian: float32 [64, 1280, 1280], P('chan', 'row'), as said below
- recoupling: float32 [64, 1280, 1280], P('chan')
- channel_size: int32 [64], P('chan'), may hold values from 128 to 1280, as said below
- hole_first: int32 [64, 1280], P('chan'), may hold values 0 or 1
- hole_second: int32 [64, 1280], P('chan'), may hold values 0 or 1
Outputs:
- derivative: float32 [64, 1280, 1280], P('chan', 'row')
Inputs may be any that keep to these rules, and one draw needn't show every extreme that they name: generator is antisymmetric and hamiltonian symmetric in every channel block. hamiltonian is symmetric in every channel block. `channel_size`: some channel has exactly 1280 states.
All inputs are finite; a program needn't handle non-finite values. No bound on the sum of `hole_first` or of `hole_second` on one device may be relied on, other than what follows from the above.
Results may differ from a plain program's by a relative error of at most 0.000076.
Values sent between devices are 32-bit elements; how exact they have to be, the bound alone decides.
No kernel may reach another device: no remote copies, remote signals or barrier semaphores. Data moves between devices by JAX's collectives and lax.ppermute only.
A program may use at most 128 MiB of HBM per device.

v0:
```python
import jax
import jax.numpy as jnp
from jax import lax
from jax.sharding import PartitionSpec as P


def batched(left, right):
    return jnp.einsum("cij,cjk->cik", left, right, precision=lax.Precision.HIGHEST)


def shards(generator, hamiltonian, recoupling, channel_size, hole_first, hole_second):
    local_count = generator.shape[0]
    row_count = generator.shape[1]
    block_order = generator.shape[2]
    chan_count = lax.axis_size("chan")
    row_index = lax.axis_index("row")
    positions = jnp.arange(block_order, dtype=jnp.int32)
    inside = (positions[None, :] < channel_size[:, None]).astype(jnp.float32)
    row_inside = lax.dynamic_slice_in_dim(inside, row_index * row_count, row_count, 1)
    block_mask = row_inside[:, :, None] * inside[:, None, :]
    gen_live = generator * block_mask
    ham_live = hamiltonian * block_mask
    weight_pp = (1 - hole_first - hole_second).astype(jnp.float32)
    weight_ph = (hole_first - hole_second).astype(jnp.float32)
    piece_shape = (local_count, row_count, chan_count, block_order // chan_count)
    gen_moved, ham_moved = (
        lax.all_to_all(
            gen_live.reshape(piece_shape), "chan", split_axis=2, concat_axis=2, tiled=True
        ),
        lax.all_to_all(
            ham_live.reshape(piece_shape), "chan", split_axis=2, concat_axis=2, tiled=True
        ),
    )
    gen_bar = batched(gen_moved.reshape(generator.shape), recoupling)
    ham_bar = batched(ham_moved.reshape(generator.shape), recoupling)
    pieces = (
        lax.all_gather(gen_bar, "row", axis=1, tiled=True),
        lax.all_gather(ham_bar, "row", axis=1, tiled=True),
    )
    factor = weight_ph[:, None, :]
    gen_cols = gen_bar * factor
    ham_cols = ham_bar * factor
    ph_term = batched(gen_cols, pieces[1]) - batched(ham_cols, pieces[0])
    turned = jnp.einsum("cij,ckj->cik", ph_term, recoupling, precision=lax.Precision.HIGHEST)
    back_moved = lax.all_to_all(
        turned.reshape(piece_shape), "chan", split_axis=2, concat_axis=2, tiled=True
    )
    ph_back = back_moved.reshape(generator.shape)
    pieces = (
        lax.all_gather(gen_live, "row", axis=1, tiled=True),
        lax.all_gather(ham_live, "row", axis=1, tiled=True),
    )
    factor = weight_pp[:, None, :]
    gen_cols = gen_live * factor
    ham_cols = ham_live * factor
    ladder = batched(gen_cols, pieces[1]) - batched(ham_cols, pieces[0])
    return (ladder + ph_back) * block_mask


def solution(mesh):
    in_specs = (
        P("chan", "row", None),
        P("chan", "row", None),
        P("chan", None, None),
        P("chan"),
        P("chan", None),
        P("chan", None),
    )
    out_specs = P("chan", "row", None)
    return jax.shard_map(shards, mesh=mesh, in_specs=in_specs, out_specs=out_specs, check_vma=False)
```

profile of v0, /device:TPU:8, one launch (start us, length us, event | category | flops | bytes accessed | tf_op | source)
XLA Modules:
  0.0 404.1 jit_solution(18243573594442668754)
XLA Ops:
  7.2 2.2 multiply_multiply_fusion.1
  9.5 3.6 copy.20
  13.0 60.7 %all_to_all.15 = f32[1,320,64,20]{1,0,3,2:T(1,128)} all-to-all(f32[1,320,64,20]{1,0,3,2:T(1,128)} %bitcast.47), channel_id=1, replica_groups=mesh['chan'=64,'row'=4] {'chan'}, dimensions={2} | all-to-all | bytes 3276800 | tf_op jit(solution)/shard_map/all_to_all | solution.py:30
  73.7 7.7 %reduce.4 = f32[320,64,20]{0,2,1:T(8,128)} reduce(f32[1,320,64,20]{1,0,3,2:T(1,128)} %all_to_all.15, f32[]{:T(128)} %constant.18), dimensions={0}, to_apply=%all_to_all.10.reduce_sub_computation | reduce | bytes 3276804 | tf_op jit(solution)/shard_map/all_to_all | solution.py:30
  81.4 2.9 reshape.159
  84.3 11.5 %fusion = f32[320,1280]{1,0:T(8,128)} fusion(f32[320,1280]{0,1:T(8,128)} %reshape.159, f32[1,1280,1280]{2,1,0:T(8,128)} %param.8), kind=kOutput, calls=%fused_computation | convolution fusion | flops 6291456000 | bytes 9830400 | tf_op jit(solution)/shard_map/cij,cjk->cik/dot_general | solution.py:8
  95.8 0.0 all-gather.13.cloned.1.call-start
  95.8 3.2 copy.19
  99.0 54.1 %all_to_all.16 = f32[1,320,64,20]{1,0,3,2:T(1,128)S(1)} all-to-all(f32[1,320,64,20]{1,0,3,2:T(1,128)} %bitcast.48), channel_id=1, replica_groups=mesh['chan'=64,'row'=4] {'chan'}, dimensions={2} | all-to-all | bytes 3276800 | tf_op jit(solution)/shard_map/all_to_all | solution.py:27
  153.1 7.0 %reduce.2 = f32[320,64,20]{0,2,1:T(8,128)} reduce(f32[1,320,64,20]{1,0,3,2:T(1,128)S(1)} %all_to_all.16, f32[]{:T(128)} %constant.18), dimensions={0}, to_apply=%all_to_all.9.reduce_sub_computation | reduce | bytes 3276804 | tf_op jit(solution)/shard_map/all_to_all | solution.py:27
  160.1 2.0 reshape.156
  162.1 10.9 %fusion.2 = f32[320,1280]{1,0:T(8,128)} fusion(f32[320,1280]{0,1:T(8,128)S(1)} %reshape.156, f32[1,1280,1280]{2,1,0:T(8,128)} %param.8), kind=kOutput, calls=%fused_computation.2 | convolution fusion | flops 6291456000 | bytes 9830400 | tf_op jit(solution)/shard_map/cij,cjk->cik/dot_general | solution.py:8
  173.0 0.0 all-gather.9.cloned.1.call-start
  173.0 0.7 all-gather.9.cloned.1.call-update
  173.7 0.0 all-gather.7.cloned.1.call-start
  173.8 0.5 all-gather.7.cloned.1.call-update
  174.3 8.4 %dot_general.37 = f32[64,20,1280]{2,1,0:T(8,128)} reshape(f32[1,1280,1280]{2,1,0:T(8,128)} %param.8) | data formatting | bytes 13107200 | tf_op jit(solution)/shard_map/cij,ckj->cik/dot_general | solution.py:44
  182.8 0.0 all-gather.11.cloned.1.call-done
  182.9 11.5 %fusion.26 = f32[320,1280]{1,0:T(8,128)} fusion(f32[1280,1280]{1,0:T(8,128)} %all-gather.11.cloned.1.call-done, f32[320,1280]{1,0:T(8,128)S(1)} %copy-done.4, f32[1280]{0:T(1024)S(1)} %get-tuple-element.6), kind=kOutput, calls=%fused_computation.21 | convolution fusion | flops 6291865600 | bytes 9835520 | tf_op jit(solution)/shard_map/cij,cjk->cik/dot_general | solution.py:8
  194.4 45.3 %all-gather.13.cloned.1.call-done = f32[1280,1280]{1,0:T(8,128)} async-done(((f32[320,1280]{1,0:T(8,128)}), f32[1280,1280]{1,0:T(8,128)}) %all-gather.13.cloned.1.call-update) | async-done | bytes 6553616 | tf_op jit(solution)/shard_map/all_gather | solution.py:37
  239.7 10.5 %fusion.19 = f32[320,1280,1]{1,0,2:T(8,128)S(1)} fusion(f32[320,1280]{1,0:T(8,128)} %fusion.26, f32[1280,1280]{1,0:T(8,128)} %all-gather.13.cloned.1.call-done, f32[320,1280]{1,0:T(8,128)S(1)} %copy-done.3, f32[1280]{0:T(1024)S(1)} %get-tuple-element.6), kind=kOutput, calls=%fused_computation.14 | convolution fusion | flops 6292275200 | bytes 11473920 | tf_op jit(solution)/shard_map/cij,cjk->cik/dot_general | solution.py:8
  250.3 11.5 %fusion.30 = f32[1,320,64,20]{1,2,3,0:T(8,128)S(1)} fusion(f32[320,1280,1]{1,0,2:T(8,128)S(1)} %fusion.19, f32[64,20,1280]{2,1,0:T(8,128)S(1)} %copy-done), kind=kOutput, calls=%fused_computation.25 | convolution fusion | flops 6291456000 | bytes 9830400 | tf_op jit(solution)/shard_map/cij,ckj->cik/dot_general | solution.py:44
  261.8 3.3 copy.22
  265.1 10.9 %all-to-all-start.2 = ((f32[1,320,64,20]{1,0,3,2:T(1,128)}), f32[1,320,64,20]{1,0,3,2:T(1,128)}, u32[]{:S(2)}, u32[]{:S(2)}) async-start(f32[1,320,64,20]{1,0,3,2:T(1,128)} %copy.22), calls=%async_computation.2 | async-start | bytes 3932160 | tf_op jit(solution)/shard_map/all_to_all | solution.py:45
  276.0 36.8 %all-gather.9.cloned.1.call-done = f32[1,1280,1280]{2,1,0:T(8,128)} async-done(((f32[1,320,1280]{2,1,0:T(8,128)}), f32[1,1280,1280]{2,1,0:T(8,128)}) %all-gather.9.cloned.1.call-update) | async-done | bytes 6553616 | tf_op jit(solution)/shard_map/all_gather | solution.py:50
  312.7 10.9 %fusion.4 = f32[320,1280]{1,0:T(8,128)} fusion(f32[1,1280,1280]{2,1,0:T(8,128)} %all-gather.9.cloned.1.call-done, f32[1,320,1280]{2,1,0:T(8,128)S(1)} %copy-done.2, f32[1280]{0:T(1024)S(1)} %get-tuple-element.5), kind=kOutput, calls=%fused_computation.4 | convolution fusion | flops 6291865600 | bytes 9835520 | tf_op jit(solution)/shard_map/cij,cjk->cik/dot_general | solution.py:8
  323.6 0.7 all-to-all-done.2
  324.4 6.3 %reduce.5 = f32[320,64,20]{0,2,1:T(8,128)S(1)} reduce(f32[1,320,64,20]{1,0,3,2:T(1,128)} %all-to-all-done.2, f32[]{:T(128)} %constant.18), dimensions={0}, to_apply=%all_to_all.11.reduce_sub_computation | reduce | bytes 3276804 | tf_op jit(solution)/shard_map/all_to_all | solution.py:45
  330.7 1.5 reshape.162
  332.2 2.2 copy.23
  334.4 51.2 %all-gather.7.cloned.1.call-done = f32[1,1280,1280]{2,1,0:T(8,128)} async-done(((f32[1,320,1280]{2,1,0:T(8,128)}), f32[1,1280,1280]{2,1,0:T(8,128)}) %all-gather.7.cloned.1.call-update) | async-done | bytes 6553616 | tf_op jit(solution)/shard_map/all_gather | solution.py:51
  385.6 11.5 %fusion.20 = f32[1,320,1280]{2,1,0:T(8,128)} fusion(f32[320,1280]{1,0:T(8,128)S(1)} %copy.23, f32[320,1280]{1,0:T(8,128)} %fusion.4, f32[1,1280,1280]{2,1,0:T(8,128)} %all-gather.7.cloned.1.call-done, f32[1280]{0:T(1024)S(1)} %fusion.37, f32[320]{0:T(512)S(1)} %fusion.38, f32[1280]{0:T(1024)S(1)} %get-tuple-element.5, f32[1,320,1280]{2,1,0:T(8,128)S(1)} %copy-done.6), kind=kOutput, calls=%fused_computation.15 | convolution fusion | flops 6294323200 | bytes 13118720 | tf_op jit(solution)/shard_map/cij,cjk->cik/dot_general | solution.py:8
  (24 shorter events, 0.1 us)
Async XLA Ops:
  6.5 176.3 %all-gather.11.cloned.1.call-start = ((), (), s32[]{:S(2)}) async-start(), calls=%async_computation.5 | async-start | bytes 8192000 | tf_op jit(solution)/shard_map/all_gather | solution.py:38
  9.4 3.6 copy-start.1
  9.5 86.4 %copy-start.5 = (f32[1,320,1280]{2,1,0:T(8,128)}, f32[1,320,1280]{2,1,0:T(8,128)S(1)}, u32[]{:S(2)}) copy-start(f32[1,320,1280]{2,1,0:T(8,128)S(1)} %get-tuple-element.7) | copy-start | bytes 4915204
  95.8 144.0 %all-gather.13.cloned.1.call-start = ((), (), s32[]{:S(2)}) async-start(), calls=%async_computation.6 | async-start | bytes 8192000 | tf_op jit(solution)/shard_map/all_gather | solution.py:37
  173.0 139.8 %all-gather.9.cloned.1.call-start = ((), (), s32[]{:S(2)}) async-start(), calls=%async_computation.4 | async-start | bytes 8192000 | tf_op jit(solution)/shard_map/all_gather | solution.py:50
  173.7 211.9 %all-gather.7.cloned.1.call-start = ((), (), s32[]{:S(2)}) async-start(), calls=%async_computation.3 | async-start | bytes 8192000 | tf_op jit(solution)/shard_map/all_gather | solution.py:51
  174.3 8.5 %copy-start.7 = (s32[1,1280]{1,0:T(1,128)S(1)}, s32[1,1280]{1,0:T(1,128)}, u32[]{:S(2)}) copy-start(s32[1,1280]{1,0:T(1,128)} %param.11) | copy-start | bytes 15364
  174.3 8.5 %copy-start.8 = (s32[1,1280]{1,0:T(1,128)S(1)}, s32[1,1280]{1,0:T(1,128)}, u32[]{:S(2)}) copy-start(s32[1,1280]{1,0:T(1,128)} %param.10) | copy-start | bytes 15364
  174.3 8.6 %copy-start.4 = (f32[320,1280]{1,0:T(8,128)S(1)}, f32[320,1280]{1,0:T(8,128)}, u32[]{:S(2)}) copy-start(f32[320,1280]{1,0:T(8,128)} %fusion.2) | copy-start | bytes 4915204
  182.9 56.9 %copy-start.3 = (f32[320,1280]{1,0:T(8,128)S(1)}, f32[320,1280]{1,0:T(8,128)}, u32[]{:S(2)}) copy-start(f32[320,1280]{1,0:T(8,128)} %fusion) | copy-start | bytes 4915204
  239.7 10.5 %copy-start = (f32[64,20,1280]{2,1,0:T(8,128)S(1)}, f32[64,20,1280]{2,1,0:T(8,128)}, u32[]{:S(2)}) copy-start(f32[64,20,1280]{2,1,0:T(8,128)} %dot_general.37) | copy-start | bytes 19660804
  265.1 47.6 %copy-start.2 = (f32[1,320,1280]{2,1,0:T(8,128)S(1)}, f32[1,320,1280]{2,1,0:T(8,128)}, u32[]{:S(2)}) copy-start(f32[1,320,1280]{2,1,0:T(8,128)} %copy-done.1) | copy-start | bytes 4915204
  265.1 59.3 %all-to-all-start.2 = ((f32[1,320,64,20]{1,0,3,2:T(1,128)}), f32[1,320,64,20]{1,0,3,2:T(1,128)}, u32[]{:S(2)}, u32[]{:S(2)}) async-start(f32[1,320,64,20]{1,0,3,2:T(1,128)} %copy.22), calls=%async_computation.2 | async-start | bytes 3932160 | tf_op jit(solution)/shard_map/all_to_all | solution.py:45
  332.2 53.4 %copy-start.6 = (f32[1,320,1280]{2,1,0:T(8,128)S(1)}, f32[1,320,1280]{2,1,0:T(8,128)}, u32[]{:S(2)}) copy-start(f32[1,320,1280]{2,1,0:T(8,128)} %param.6) | copy-start | bytes 4915204
Sparse Core Ops, SparseCore 0:
  95.9 66.6 all-gather.10
  173.1 66.6 all-gather.12
  241.6 71.1 all-gather.8
  314.4 71.1 all-gather.6
where the time goes:
time: 411 us; the launch traced here: 404 us
  waiting for transfers between devices  135 us (33%)
  blocking collectives  115 us (28%)
  matrix products  78.3 us (19%)
  local copies, waits for them, and re-layouts  27 us (7%)
  other arithmetic  23.3 us (6%)
  between operations  14.4 us (4%)
  starting transfers between devices  11 us (3%)
    dot_general x6, matrix products, batched(): jnp.einsum('cij,cjk->cik', left, right, precision=lax.Precision.HIGHEST)  66.8 us
    all_to_all x1, blocking collectives, shards(): lax.all_to_all(ham_live.reshape(piece_shape), 'chan', split_axis=2, conca...  60.7 us
    all_to_all x1, blocking collectives, shards(): lax.all_to_all(gen_live.reshape(piece_shape), 'chan', split_axis=2, conca...  54.1 us
    all_gather x1, waiting for transfers between devices, shards(): lax.all_gather(ham_live, 'row', axis=1, tiled=True)  51.2 us
    all_gather x1, waiting for transfers between devices, shards(): lax.all_gather(gen_bar, 'row', axis=1, tiled=True)  45.3 us
    all_gather x1, waiting for transfers between devices, shards(): lax.all_gather(gen_live, 'row', axis=1, tiled=True)  36.8 us
    dot_general x2, local copies, waits for them, and re-layouts, shards(): jnp.einsum('cij,ckj->cik', ph_term, recoupling, precision=lax.Precision.H...  11.7 us
    dot_general x1, matrix products, shards(): jnp.einsum('cij,ckj->cik', ph_term, recoupling, precision=lax.Precision.H...  11.5 us
  transfers between devices with their start and end apart: 5, of which 4 were waited for; matrix products, arithmetic and copies ran while one was open for 22% of the time, Pallas kernels for 0%

commit v1 on v0

v1 whole, which is shorter than its diff:
```python
import functools

import jax
import jax.numpy as jnp
from jax import lax
from jax.experimental import pallas as pl
from jax.experimental.pallas import tpu as pltpu
from jax.sharding import PartitionSpec as P

F32 = jnp.float32
BF16 = jnp.bfloat16
VMEM_LIMIT = 56 * 1024 * 1024
NN = ((1,), (0,))
NT = ((1,), (1,))
TILE = 256
LANES = 128


def split(x):
    high = x.astype(BF16)
    return high, (x - high.astype(F32)).astype(BF16)


def dot3(a, b, dims):
    def one(left, right):
        return lax.dot_general(left, right, (dims, ((), ())), preferred_element_type=F32)

    return one(a[0], b[0]) + (one(a[0], b[1]) + one(a[1], b[0]))


def call(kernel, out_shape, flops, **kwargs):
    return pl.pallas_call(
        kernel,
        out_shape=out_shape,
        compiler_params=pltpu.CompilerParams(vmem_limit_bytes=VMEM_LIMIT),
        cost_estimate=pl.CostEstimate(flops=flops, bytes_accessed=8_000_000, transcendentals=0),
        **kwargs,
    )


def whole(shape):
    return pl.BlockSpec(shape, lambda *_: (0,) * len(shape))


SMEM = pl.BlockSpec(memory_space=pltpu.SMEM)


def pack(source, target, count, width):
    rows = source.shape[1]
    half = width // 2
    body = rows // LANES * LANES

    def pair(step, _):
        block = source[pl.ds(pl.multiple_of(step * 2 * width, 8), 2 * width), :]
        for odd in range(2):
            part = block[odd * width : (odd + 1) * width]
            at = 0
            for lane in range(0, body, LANES):
                target[2 * step + odd, at : at + width, :] = part[:, lane : lane + LANES]
                at += width
            target[2 * step + odd, at : at + half, :] = jnp.concatenate(
                [part[:half, body:], part[half:, body:]], axis=1
            )
        return 0

    lax.fori_loop(0, count // 2, pair, 0)


def unpack(source, target, count, width):
    rows = target.shape[1]
    half = width // 2
    body = rows // LANES * LANES
    rest = rows - body

    def pair(step, _):
        parts = []
        for odd in range(2):
            at = 0
            columns = []
            for lane in range(0, body, LANES):
                columns.append(source[2 * step + odd, at : at + width, :])
                at += width
            tail = source[2 * step + odd, at : at + half, :]
            columns.append(jnp.concatenate([tail[:, :rest], tail[:, rest:]], axis=0))
            parts.append(jnp.concatenate(columns, axis=1))
        target[pl.ds(pl.multiple_of(step * 2 * width, 8), 2 * width), :] = jnp.concatenate(parts, axis=0)
        return 0

    lax.fori_loop(0, count // 2, pair, 0)


def encode_kernel(count, width, where_ref, x_ref, out_ref, turned):
    rows, order = x_ref.shape
    size, row_index = where_ref[0], where_ref[1]
    for start in range(0, order, TILE):
        block = x_ref[:, start : start + TILE]
        row = lax.broadcasted_iota(jnp.int32, block.shape, 0) + row_index * rows
        column = lax.broadcasted_iota(jnp.int32, block.shape, 1) + start
        live = jnp.where((row < size) & (column < size), block, 0.0)
        turned[start : start + TILE, :] = live.T
    pack(turned, out_ref, count, width)


def encode(x, where, count):
    rows, order = x.shape
    width = order // count
    depth = -(-(rows * width // LANES) // 8) * 8
    return call(
        functools.partial(encode_kernel, count, width),
        jax.ShapeDtypeStruct((count, depth, LANES), F32),
        1000,
        in_specs=[SMEM, whole(x.shape)],
        out_specs=whole((count, depth, LANES)),
        scratch_shapes=[pltpu.VMEM((order, rows), F32)],
        grid=(1,),
    )(where, x)


def bar_kernel(count, width, message_ref, recouple_ref, out_ref, turned, high, low):
    order = recouple_ref.shape[0]

    @pl.when(pl.program_id(0) == 0)
    def _():
        unpack(message_ref, turned, count, width)
        for start in range(0, order, TILE):
            piece = split(turned[start : start + TILE, :].T)
            high[:, start : start + TILE] = piece[0]
            low[:, start : start + TILE] = piece[1]

    out_ref[...] = dot3((high[...], low[...]), split(recouple_ref[...]), NN)


def bar(message, recoupling, rows):
    order = recoupling.shape[0]
    count = message.shape[0]
    return call(
        functools.partial(bar_kernel, count, order // count),
        jax.ShapeDtypeStruct((rows, order), F32),
        6 * rows * order * order,
        in_specs=[whole(message.shape), pl.BlockSpec((order, TILE), lambda n: (0, n))],
        out_specs=pl.BlockSpec((rows, TILE), lambda n: (0, n)),
        scratch_shapes=[
            pltpu.VMEM((order, rows), F32),
            pltpu.VMEM((rows, order), BF16),
            pltpu.VMEM((rows, order), BF16),
        ],
        grid=(order // TILE,),
    )(message, recoupling)


def ladder_kernel(where_ref, gen_ref, ham_ref, first_ref, second_ref, out_ref, left_high, left_low, right_high, right_low):
    rows, order = gen_ref.shape
    size, row_index = where_ref[0], where_ref[1]

    @pl.when(pl.program_id(0) == 0)
    def _():
        position = lax.broadcasted_iota(jnp.int32, (1, order), 1)
        weight = jnp.where(position < size, (first_ref[...] + second_ref[...] - 1).astype(F32), 0.0)
        mine = weight[:, :rows]
        for other in range(1, order // rows):
            mine = jnp.where(row_index == other, weight[:, other * rows : (other + 1) * rows], mine)
        for place, (left, right) in enumerate(((gen_ref, ham_ref), (ham_ref, gen_ref))):
            span = slice(place * rows, (place + 1) * rows)
            for start in range(0, order, TILE):
                piece = split(left[:, start : start + TILE].T * mine)
                left_high[start : start + TILE, span] = piece[0]
                left_low[start : start + TILE, span] = piece[1]
            right_high[span, :], right_low[span, :] = split(right[...])

    columns = pl.ds(pl.multiple_of(pl.program_id(0) * TILE, TILE), TILE)
    out_ref[...] = dot3((left_high[...], left_low[...]), (right_high[:, columns], right_low[:, columns]), NN)


def ladder_part(gen, ham, first, second, where):
    rows, order = gen.shape
    return call(
        ladder_kernel,
        jax.ShapeDtypeStruct((order, order), F32),
        12 * rows * order * order,
        in_specs=[SMEM, whole(gen.shape), whole(gen.shape), whole((1, order)), whole((1, order))],
        out_specs=pl.BlockSpec((order, TILE), lambda n: (0, n)),
        scratch_shapes=[pltpu.VMEM((order, 2 * rows), BF16)] * 2 + [pltpu.VMEM((2 * rows, order), BF16)] * 2,
        grid=(order // TILE,),
    )(where, gen, ham, first, second)


def commutator_kernel(gen_ref, ham_ref, first_ref, second_ref, gen_all, ham_all, out_ref, gen_high, gen_low, ham_high, ham_low):
    @pl.when(pl.program_id(0) == 0)
    def _():
        weight = (first_ref[...] - second_ref[...]).astype(F32)
        gen_high[...], gen_low[...] = split(gen_ref[...] * weight)
        ham_high[...], ham_low[...] = split(ham_ref[...] * weight)

    out_ref[...] = dot3((gen_high[...], gen_low[...]), split(ham_all[...]), NN) - dot3(
        (ham_high[...], ham_low[...]), split(gen_all[...]), NN
    )


def commutator(gen, ham, first, second, gen_all, ham_all):
    rows, order = gen.shape
    tall = pl.BlockSpec((order, TILE), lambda n: (0, n))
    return call(
        commutator_kernel,
        jax.ShapeDtypeStruct((rows, order), F32),
        12 * rows * order * order,
        in_specs=[whole(gen.shape), whole(gen.shape), whole((1, order)), whole((1, order)), tall, tall],
        out_specs=pl.BlockSpec((rows, TILE), lambda n: (0, n)),
        scratch_shapes=[pltpu.VMEM((rows, order), BF16)] * 4,
        grid=(order // TILE,),
    )(gen, ham, first, second, gen_all, ham_all)


def turn_kernel(count, width, term_ref, recouple_ref, out_ref, high, low, turned):
    @pl.when(pl.program_id(0) == 0)
    def _():
        high[...], low[...] = split(term_ref[...])

    turned[...] = dot3(split(recouple_ref[...]), (high[...], low[...]), NT)
    pack(turned, out_ref, count, width)


def turn(term, recoupling, count):
    rows, order = term.shape
    width = order // count
    steps = 4
    depth = -(-(rows * width // LANES) // 8) * 8
    return call(
        functools.partial(turn_kernel, count // steps, width),
        jax.ShapeDtypeStruct((count, depth, LANES), F32),
        6 * rows * order * order,
        in_specs=[whole(term.shape), pl.BlockSpec((order // steps, order), lambda n: (n, 0))],
        out_specs=pl.BlockSpec((count // steps, depth, LANES), lambda n: (n, 0, 0)),
        scratch_shapes=[
            pltpu.VMEM((rows, order), BF16),
            pltpu.VMEM((rows, order), BF16),
            pltpu.VMEM((order // steps, rows), F32),
        ],
        grid=(steps,),
    )(term, recoupling)


def finish_kernel(count, width, where_ref, message_ref, ladder_ref, out_ref, turned):
    rows, order = out_ref.shape
    size, row_index = where_ref[0], where_ref[1]
    unpack(message_ref, turned, count, width)
    for start in range(0, order, TILE):
        span = slice(start, start + TILE)
        total = ladder_ref[:, span] + turned[span, :].T
        row = lax.broadcasted_iota(jnp.int32, total.shape, 0) + row_index * rows
        column = lax.broadcasted_iota(jnp.int32, total.shape, 1) + start
        out_ref[:, span] = jnp.where((row < size) & (column < size), total, 0.0)


def finish(message, ladder, where):
    rows, order = ladder.shape
    count = message.shape[0]
    return call(
        functools.partial(finish_kernel, count, order // count),
        jax.ShapeDtypeStruct((rows, order), F32),
        1000,
        in_specs=[SMEM, whole(message.shape), whole(ladder.shape)],
        out_specs=whole(ladder.shape),
        scratch_shapes=[pltpu.VMEM((order, rows), F32)],
        grid=(1,),
    )(where, message, ladder)


def exchange(message):
    return lax.all_to_all(message, "chan", 0, 0, tiled=True)


def gather(x):
    return lax.all_gather(x, "row", axis=0, tiled=True)


def shards(generator, hamiltonian, recoupling, channel_size, hole_first, hole_second):
    gen, ham, recouple = generator[0], hamiltonian[0], recoupling[0]
    rows = gen.shape[0]
    count = lax.axis_size("chan")
    where = jnp.stack([channel_size[0], lax.axis_index("row").astype(jnp.int32)])
    gen_moved = exchange(encode(gen, where, count))
    ham_moved = exchange(encode(ham, where, count))
    part = ladder_part(gen, ham, hole_first, hole_second, where)
    ladder = lax.psum_scatter(part, "row", scatter_dimension=0, tiled=True)
    gen_bar = bar(gen_moved, recouple, rows)
    gen_all = gather(gen_bar)
    ham_bar = bar(ham_moved, recouple, rows)
    ham_all = gather(ham_bar)
    term = commutator(gen_bar, ham_bar, hole_first, hole_second, gen_all, ham_all)
    back = exchange(turn(term, recouple, count))
    return finish(back, ladder, where)[None]


def solution(mesh):
    in_specs = (
        P("chan", "row", None),
        P("chan", "row", None),
        P("chan", None, None),
        P("chan"),
        P("chan", None),
        P("chan", None),
    )
    out_specs = P("chan", "row", None)
    return jax.shard_map(shards, mesh=mesh, in_specs=in_specs, out_specs=out_specs, check_vma=False)
```

time: 411 us -> 316 us (0.77); the launches traced: 404 us -> 315 us
  matrix products: 78.3 us -> 0 us
  Pallas kernels: 0 us -> 77.6 us
  waiting for transfers between devices: 135 us -> 102 us
  local copies, waits for them, and re-layouts: 27 us -> 1.25 us
  other arithmetic: 23.3 us -> 0.65 us
  blocking collectives: 115 us -> 109 us
    dot_general x7 -> x0, matrix products: 78.3 us -> none  [the longest x6 66.8 us: batched(): jnp.einsum('cij,cjk->cik', left, right, precision=lax.Precision.HIGHEST)]
    pallas_call x0 -> x8, Pallas kernels: none -> 77.6 us  [the longest x2 21.9 us: bar(): call(functools.partial(bar_kernel, count, order // count), jax.ShapeDtype...]
    all_gather x4 -> x2, waiting for transfers between devices: 133 us -> 56.7 us  [gather(): return lax.all_gather(x, 'row', axis=0, tiled=True)]
    reduce_scatter x0 -> x1, waiting for transfers between devices: none -> 38.1 us  [shards(): ladder = lax.psum_scatter(part, 'row', scatter_dimension=0, tiled=True)]
    all_to_all x3 -> x0, other arithmetic: 21 us -> none  [the longest x1 7.73 us: shards(): lax.all_to_all(ham_live.reshape(piece_shape), 'chan', split_axis=2, conca...]
    dot_general x2 -> x0, local copies, waits for them, and re-layouts: 11.7 us -> none  [shards(): jnp.einsum('cij,ckj->cik', ph_term, recoupling, precision=lax.Precision.H...]
    all_to_all x1, waiting for transfers between devices: 0.74 us -> 7.5 us  [exchange(): return lax.all_to_all(message, 'chan', 0, 0, tiled=True)]
    mul x2 -> x0, local copies, waits for them, and re-layouts: 6.75 us -> none  [the longest x1 3.57 us: shards(): ham_live = hamiltonian * block_mask]
  transfers between devices with their start and end apart: 5 -> 4, of which waited for: 4 -> 3; matrix products, arithmetic and copies ran while one was open for 22% -> 0% of each run, Pallas kernels for 0% -> 17%
where the time goes in v1:
time: 316 us; the launch traced here: 315 us
  blocking collectives  109 us (34%)
  waiting for transfers between devices  102 us (32%)
  Pallas kernels  77.6 us (25%)
  between operations  13.8 us (4%)
  starting transfers between devices  10.8 us (3%)
    all_to_all x2, blocking collectives, exchange(): return lax.all_to_all(message, 'chan', 0, 0, tiled=True)  109 us
    all_gather x2, waiting for transfers between devices, gather(): return lax.all_gather(x, 'row', axis=0, tiled=True)  56.7 us
    reduce_scatter x1, waiting for transfers between devices, shards(): ladder = lax.psum_scatter(part, 'row', scatter_dimension=0, tiled=True)  38.1 us
    pallas_call x2, Pallas kernels, bar(): call(functools.partial(bar_kernel, count, order // count), jax.ShapeDtype...  21.9 us
    pallas_call x1, Pallas kernels, ladder_part(): call(ladder_kernel, jax.ShapeDtypeStruct((order, order), F32), 12 * rows...  14.8 us
    pallas_call x1, Pallas kernels, commutator(): call(commutator_kernel, jax.ShapeDtypeStruct((rows, order), F32), 12 * ro...  12.2 us
    pallas_call x2, Pallas kernels, encode(): call(functools.partial(encode_kernel, count, width), jax.ShapeDtypeStruct...  11.5 us
    pallas_call x1, Pallas kernels, turn(): call(functools.partial(turn_kernel, count // steps, width), jax.ShapeDtyp...  11.1 us
  transfers between devices with their start and end apart: 4, of which 3 were waited for; matrix products, arithmetic and copies ran while one was open for 0% of the time, Pallas kernels for 17%

profile of v1, /device:TPU:8, one launch (start us, length us, event | category | flops | bytes accessed | tf_op | source)
XLA Modules:
  0.0 315.5 jit_solution(13603666205313354981)
XLA Ops:
  6.5 0.0 all-gather.3.cloned.1.call-start
  7.2 0.6 pad_add_fusion.where_ref
  7.8 5.7 %shard_map.64 = f32[64,56,128]{2,1,0:T(8,128)} custom-call(s32[2]{0:T(128)} %pad_add_fusion.where_ref, f32[320,1280]{1,0:T(8,128)} %bitcast.5), custom_call_target="tpu_custom_call" | custom-call | flops 1000 | bytes 8000000 | tf_op jit(solution)/shard_map/pallas_call | solution.py:108
  13.6 57.9 %all_to_all.15.message_ref = f32[64,56,128]{2,1,0:T(8,128)} all-to-all(f32[64,56,128]{2,1,0:T(8,128)} %shard_map.64), channel_id=1, replica_groups=mesh['chan'=64,'row'=4] {'chan'}, dimensions={0} | all-to-all | bytes 3670016 | tf_op jit(solution)/shard_map/all_to_all | solution.py:269
  71.4 10.9 %shard_map.65.gen_ref = f32[320,1280]{1,0:T(8,128)} custom-call(f32[64,56,128]{2,1,0:T(8,128)} %all_to_all.15.message_ref, f32[1280,1280]{1,0:T(8,128)} %bitcast.9), custom_call_target="tpu_custom_call" | custom-call | flops 3145728000 | bytes 8000000 | tf_op jit(solution)/shard_map/pallas_call | solution.py:136
  82.4 0.0 all-gather.3.cloned.1.call-update
  82.4 0.0 all-gather.5.cloned.1.call-start
  82.4 5.8 %shard_map.66 = f32[64,56,128]{2,1,0:T(8,128)} custom-call(s32[2]{0:T(128)} %pad_add_fusion.where_ref, f32[320,1280]{1,0:T(8,128)} %bitcast.7), custom_call_target="tpu_custom_call" | custom-call | flops 1000 | bytes 8000000 | tf_op jit(solution)/shard_map/pallas_call | solution.py:108
  88.2 51.2 %all_to_all.16.message_ref = f32[64,56,128]{2,1,0:T(8,128)} all-to-all(f32[64,56,128]{2,1,0:T(8,128)} %shard_map.66), channel_id=1, replica_groups=mesh['chan'=64,'row'=4] {'chan'}, dimensions={0} | all-to-all | bytes 3670016 | tf_op jit(solution)/shard_map/all_to_all | solution.py:269
  139.4 11.0 %shard_map.67.ham_ref = f32[320,1280]{1,0:T(8,128)} custom-call(f32[64,56,128]{2,1,0:T(8,128)} %all_to_all.16.message_ref, f32[1280,1280]{1,0:T(8,128)} %bitcast.10), custom_call_target="tpu_custom_call" | custom-call | flops 3145728000 | bytes 8000000 | tf_op jit(solution)/shard_map/pallas_call | solution.py:136
  150.4 0.0 all-gather.5.cloned.1.call-update
  150.4 0.2 reduce-scatter.2.cloned.1.call-start
  150.6 14.8 %shard_map.70 = f32[1280,1280]{1,0:T(8,128)} custom-call(s32[2]{0:T(128)} %pad_add_fusion.where_ref, f32[320,1280]{1,0:T(8,128)} %bitcast.6, f32[320,1280]{1,0:T(8,128)} %bitcast.8, s32[1,1280]{1,0:T(1,128)} %first_ref.3, s32[1,1280]{1,0:T(1,128)} %second_ref.3), custom_call_target="tpu_custom_call" | custom-call | flops 6291456000 | bytes 8000000 | tf_op jit(solution)/shard_map/pallas_call | solution.py:176
  165.5 0.0 reduce-scatter.2.cloned.1.call-update
  165.5 0.0 all-gather.3.cloned.1.call-done.gen_all
  165.5 56.6 %all-gather.5.cloned.1.call-done.ham_all = f32[1280,1280]{1,0:T(8,128)} async-done(((f32[320,1280]{1,0:T(8,128)}), f32[1280,1280]{1,0:T(8,128)}) %all-gather.5.cloned.1.call-update) | async-done | bytes 6553616 | tf_op jit(solution)/shard_map/all_gather | solution.py:273
  222.1 12.2 %shard_map.68.term_ref = f32[320,1280]{1,0:T(8,128)} custom-call(f32[320,1280]{1,0:T(8,128)} %shard_map.65.gen_ref, f32[320,1280]{1,0:T(8,128)} %shard_map.67.ham_ref, s32[1,1280]{1,0:T(1,128)} %first_ref.3, s32[1,1280]{1,0:T(1,128)} %second_ref.3, f32[1280,1280]{1,0:T(8,128)} %all-gather.3.cloned.1.call-done.gen_all, ...), custom_call_target="tpu_custom_call" | custom-call | flops 6291456000 | bytes 8000000 | tf_op jit(solution)/shard_map/pallas_call | solution.py:202
  234.3 11.1 %shard_map.69 = f32[64,56,128]{2,1,0:T(8,128)} custom-call(f32[320,1280]{1,0:T(8,128)} %shard_map.68.term_ref, f32[1280,1280]{1,0:T(8,128)} %bitcast.11), custom_call_target="tpu_custom_call" | custom-call | flops 3145728000 | bytes 8000000 | tf_op jit(solution)/shard_map/pallas_call | solution.py:227
  245.4 10.6 %all-to-all-start.2 = ((f32[64,56,128]{2,1,0:T(8,128)}), f32[64,56,128]{2,1,0:T(8,128)S(1)}, u32[]{:S(2)}, u32[]{:S(2)}) async-start(f32[64,56,128]{2,1,0:T(8,128)} %shard_map.69), calls=%async_computation.2 | async-start | bytes 3670016 | tf_op jit(solution)/shard_map/all_to_all | solution.py:269
  255.9 38.1 %reduce-scatter.2.cloned.1.call-done.ladder_ref = f32[320,1280]{1,0:T(8,128)} async-done(((f32[1280,1280]{1,0:T(8,128)}), f32[320,1280]{1,0:T(8,128)}) %reduce-scatter.2.cloned.1.call-update) | async-done | bytes 1638416 | tf_op jit(solution)/shard_map/reduce_scatter | solution.py:284
  294.1 7.5 %all-to-all-done.2.message_ref = f32[64,56,128]{2,1,0:T(8,128)S(1)} async-done(((f32[64,56,128]{2,1,0:T(8,128)}), f32[64,56,128]{2,1,0:T(8,128)S(1)}, u32[]{:S(2)}, u32[]{:S(2)}) %all-to-all-start.2) | async-done | bytes 1835040 | tf_op jit(solution)/shard_map/all_to_all | solution.py:269
  301.6 0.0 copy-start
  301.6 1.2 copy-done
  302.8 6.1 %shard_map.71 = f32[320,1280]{1,0:T(8,128)} custom-call(s32[2]{0:T(128)} %pad_add_fusion.where_ref, f32[64,56,128]{2,1,0:T(8,128)} %copy-done, f32[320,1280]{1,0:T(8,128)} %reduce-scatter.2.cloned.1.call-done.ladder_ref), custom_call_target="tpu_custom_call" | custom-call | flops 1000 | bytes 8000000 | tf_op jit(solution)/shard_map/pallas_call | solution.py:257
Async XLA Ops:
  6.5 159.0 %all-gather.3.cloned.1.call-start = ((), (), s32[]{:S(2)}) async-start(), calls=%async_computation.4 | async-start | bytes 8192000 | tf_op jit(solution)/shard_map/all_gather | solution.py:273
  82.4 139.8 %all-gather.5.cloned.1.call-start = ((), (), s32[]{:S(2)}) async-start(), calls=%async_computation.5 | async-start | bytes 8192000 | tf_op jit(solution)/shard_map/all_gather | solution.py:273
  150.4 143.7 %reduce-scatter.2.cloned.1.call-start = ((), (), s32[]{:S(2)}) async-start(), calls=%async_computation.6 | async-start | bytes 8192000 | tf_op jit(solution)/shard_map/reduce_scatter | solution.py:284
  245.4 56.2 %all-to-all-start.2 = ((f32[64,56,128]{2,1,0:T(8,128)}), f32[64,56,128]{2,1,0:T(8,128)S(1)}, u32[]{:S(2)}, u32[]{:S(2)}) async-start(f32[64,56,128]{2,1,0:T(8,128)} %shard_map.69), calls=%async_computation.2 | async-start | bytes 3670016 | tf_op jit(solution)/shard_map/all_to_all | solution.py:269
  301.6 1.2 copy-start
Sparse Core Ops, SparseCore 0:
  82.5 66.6 all-gather.2
  151.0 71.1 all-gather.4
  224.7 69.3 reduce-scatter.1

commit v2 on v1

v2 whole, which is shorter than its diff:
```python
import functools

import jax
import jax.numpy as jnp
from jax import lax
from jax.experimental import pallas as pl
from jax.experimental.pallas import tpu as pltpu
from jax.sharding import PartitionSpec as P

F32 = jnp.float32
BF16 = jnp.bfloat16
VMEM_LIMIT = 56 * 1024 * 1024
NN = ((1,), (0,))
NT = ((1,), (1,))
TILE = 256
LANES = 128
FAST = 1000


def split(x):
    high = x.astype(BF16)
    return high, (x - high.astype(F32)).astype(BF16)


def dot3(a, b, dims):
    def one(left, right):
        return lax.dot_general(left, right, (dims, ((), ())), preferred_element_type=F32)

    return one(a[0], b[0]) + (one(a[0], b[1]) + one(a[1], b[0]))


def call(kernel, out_shape, flops, inputs, in_specs, after=(), **kwargs):
    first, last = len(inputs), len(inputs) + len(after)

    def body(*refs):
        kernel(*refs[:first], *refs[last:])

    return pl.pallas_call(
        body,
        out_shape=out_shape,
        in_specs=list(in_specs) + [pl.BlockSpec(memory_space=pl.ANY)] * len(after),
        compiler_params=pltpu.CompilerParams(vmem_limit_bytes=VMEM_LIMIT),
        cost_estimate=pl.CostEstimate(flops=flops, bytes_accessed=8_000_000, transcendentals=0),
        **kwargs,
    )(*inputs, *after)


def whole(shape):
    return pl.BlockSpec(shape, lambda *_: (0,) * len(shape))


SMEM = pl.BlockSpec(memory_space=pltpu.SMEM)


def pack(source, target, count, width):
    rows = source.shape[1]
    half = width // 2
    body = rows // LANES * LANES

    def pair(step, _):
        block = source[pl.ds(pl.multiple_of(step * 2 * width, 8), 2 * width), :]
        for odd in range(2):
            part = block[odd * width : (odd + 1) * width]
            at = 0
            for lane in range(0, body, LANES):
                target[2 * step + odd, at : at + width, :] = part[:, lane : lane + LANES]
                at += width
            target[2 * step + odd, at : at + half, :] = jnp.concatenate(
                [part[:half, body:], part[half:, body:]], axis=1
            )
        return 0

    lax.fori_loop(0, count // 2, pair, 0)


def unpack(source, target, count, width):
    rows = target.shape[1]
    half = width // 2
    body = rows // LANES * LANES
    rest = rows - body

    def pair(step, _):
        parts = []
        for odd in range(2):
            at = 0
            columns = []
            for lane in range(0, body, LANES):
                columns.append(source[2 * step + odd, at : at + width, :])
                at += width
            tail = source[2 * step + odd, at : at + half, :]
            columns.append(jnp.concatenate([tail[:, :rest], tail[:, rest:]], axis=0))
            parts.append(jnp.concatenate(columns, axis=1))
        target[pl.ds(pl.multiple_of(step * 2 * width, 8), 2 * width), :] = jnp.concatenate(parts, axis=0)
        return 0

    lax.fori_loop(0, count // 2, pair, 0)


def encode_kernel(count, width, where_ref, x_ref, out_ref, turned):
    rows, order = x_ref.shape
    size, row_index = where_ref[0], where_ref[1]
    for start in range(0, order, TILE):
        block = x_ref[:, start : start + TILE]
        row = lax.broadcasted_iota(jnp.int32, block.shape, 0) + row_index * rows
        column = lax.broadcasted_iota(jnp.int32, block.shape, 1) + start
        live = jnp.where((row < size) & (column < size), block, 0.0)
        turned[start : start + TILE, :] = live.T
    pack(turned, out_ref, count, width)


def encode(x, where, count, after=()):
    rows, order = x.shape
    width = order // count
    depth = -(-(rows * width // LANES) // 8) * 8
    return call(
        functools.partial(encode_kernel, count, width),
        jax.ShapeDtypeStruct((count, depth, LANES), F32),
        FAST,
        (where, x),
        [SMEM, whole(x.shape)],
        after,
        out_specs=whole((count, depth, LANES)),
        scratch_shapes=[pltpu.VMEM((order, rows), F32)],
        grid=(1,),
    )


def bar_kernel(count, width, message_ref, recouple_ref, *refs):
    outs, (turned, high, low) = refs[:-3], refs[-3:]
    order = recouple_ref.shape[0]

    @pl.when(pl.program_id(0) == 0)
    def _():
        unpack(message_ref, turned, count, width)
        for start in range(0, order, TILE):
            piece = split(turned[start : start + TILE, :].T)
            high[:, start : start + TILE] = piece[0]
            low[:, start : start + TILE] = piece[1]

    product = dot3((high[...], low[...]), split(recouple_ref[...]), NN)
    if len(outs) == 1:
        outs[0][...] = product
        return
    for step, out in enumerate(outs):

        @pl.when(pl.program_id(0) == step)
        def _():
            out[...] = product


def bar(message, recoupling, rows, halves, after=()):
    order = recoupling.shape[0]
    count = message.shape[0]
    tile = order // 2 if halves else TILE
    if halves:
        out_shape = [jax.ShapeDtypeStruct((rows, tile), F32)] * 2
        out_specs = [whole((rows, tile))] * 2
    else:
        out_shape = jax.ShapeDtypeStruct((rows, order), F32)
        out_specs = pl.BlockSpec((rows, TILE), lambda n: (0, n))
    return call(
        functools.partial(bar_kernel, count, order // count),
        out_shape,
        6 * rows * order * order,
        (message, recoupling),
        [whole(message.shape), pl.BlockSpec((order, tile), lambda n: (0, n))],
        after,
        out_specs=out_specs,
        scratch_shapes=[
            pltpu.VMEM((order, rows), F32),
            pltpu.VMEM((rows, order), BF16),
            pltpu.VMEM((rows, order), BF16),
        ],
        grid=(order // tile,),
    )


def ladder_kernel(cut, where_ref, gen_ref, ham_ref, first_ref, second_ref, early_ref, late_ref, left_high, left_low, right_high, right_low):
    rows, order = gen_ref.shape
    size, row_index = where_ref[0], where_ref[1]
    step = pl.program_id(0)

    @pl.when(step == 0)
    def _():
        position = lax.broadcasted_iota(jnp.int32, (1, order), 1)
        weight = jnp.where(position < size, (first_ref[...] + second_ref[...] - 1).astype(F32), 0.0)
        mine = weight[:, :rows]
        for other in range(1, order // rows):
            mine = jnp.where(row_index == other, weight[:, other * rows : (other + 1) * rows], mine)
        for place, (left, right) in enumerate(((gen_ref, ham_ref), (ham_ref, gen_ref))):
            span = slice(place * rows, (place + 1) * rows)
            for start in range(0, order, TILE):
                piece = split(left[:, start : start + TILE].T * mine)
                left_high[start : start + TILE, span] = piece[0]
                left_low[start : start + TILE, span] = piece[1]
            right_high[span, :], right_low[span, :] = split(right[...])

    columns = pl.ds(pl.multiple_of(step * TILE, TILE), TILE)
    product = dot3((left_high[...], left_low[...]), (right_high[:, columns], right_low[:, columns]), NN)

    @pl.when(step < cut)
    def _():
        early_ref[...] = product

    @pl.when(step >= cut)
    def _():
        late_ref[...] = product


def ladder_part(gen, ham, first, second, where, after=()):
    rows, order = gen.shape
    steps = order // TILE
    cut = steps // 2
    return call(
        functools.partial(ladder_kernel, cut),
        [
            jax.ShapeDtypeStruct((order, cut * TILE), F32),
            jax.ShapeDtypeStruct((order, (steps - cut) * TILE), F32),
        ],
        12 * rows * order * order,
        (where, gen, ham, first, second),
        [SMEM, whole(gen.shape), whole(gen.shape), whole((1, order)), whole((1, order))],
        after,
        out_specs=[
            pl.BlockSpec((order, TILE), lambda n: (0, jnp.minimum(n, cut - 1))),
            pl.BlockSpec((order, TILE), lambda n: (0, jnp.maximum(n - cut, 0))),
        ],
        scratch_shapes=[pltpu.VMEM((order, 2 * rows), BF16)] * 2 + [pltpu.VMEM((2 * rows, order), BF16)] * 2,
        grid=(steps,),
    )


def weighted(first_ref, second_ref):
    return (first_ref[...] - second_ref[...]).astype(F32)


def local_kernel(gen_all, low_ref, high_ref, first_ref, second_ref, out_ref, ham_high, ham_low):
    half = low_ref.shape[1]

    @pl.when(pl.program_id(0) == 0)
    def _():
        weight = weighted(first_ref, second_ref)
        for place, ref in enumerate((low_ref, high_ref)):
            span = slice(place * half, (place + 1) * half)
            ham_high[:, span], ham_low[:, span] = split(ref[...] * weight[:, span])

    out_ref[...] = dot3((ham_high[...], ham_low[...]), split(gen_all[...]), NN)


def local_term(gen_all, ham_halves, first, second, after=()):
    rows, half = ham_halves[0].shape
    order = 2 * half
    return call(
        local_kernel,
        jax.ShapeDtypeStruct((rows, order), F32),
        6 * rows * order * order,
        (gen_all, *ham_halves, first, second),
        [pl.BlockSpec((order, TILE), lambda n: (0, n))]
        + [whole((rows, half))] * 2
        + [whole((1, order))] * 2,
        after,
        out_specs=pl.BlockSpec((rows, TILE), lambda n: (0, n)),
        scratch_shapes=[pltpu.VMEM((rows, order), BF16)] * 2,
        grid=(order // TILE,),
    )


def pair_kernel(pick_ref, gen_ref, own_ref, got_ref, first_ref, second_ref, out_ref, right_high, right_low):
    rows, order = gen_ref.shape
    half = order // 2
    kind = pick_ref[2]
    scaled = gen_ref[...] * weighted(first_ref, second_ref)
    outer = jnp.concatenate([scaled[:, :rows], scaled[:, order - rows :]], axis=1)
    inner = scaled[:, rows : order - rows]
    ends = jnp.where(kind == 2, scaled[:, :half], scaled[:, half:])
    left = split(jnp.where(kind == 0, outer, jnp.where(kind == 1, inner, ends)))
    own_at = pl.multiple_of(pick_ref[1], 64)
    got_at = pl.multiple_of(rows - pick_ref[1], 64)
    for at, ref in ((own_at, own_ref), (got_at, got_ref)):
        right_high[pl.ds(at, rows), :], right_low[pl.ds(at, rows), :] = split(ref[...])
    out_ref[...] = dot3(left, (right_high[...], right_low[...]), NN)


def pair_product(pick, gen_all, own, got, first, second, after=()):
    rows, half = own.shape
    order = 2 * half
    inputs = (gen_all, own, got, first, second)
    count = 1 + len(inputs)

    def body(*refs):
        pair_kernel(*refs[:count], *refs[count + len(after) :])

    def fixed(shape):
        return pl.BlockSpec(shape, lambda n, pick: (0, 0))

    return pl.pallas_call(
        body,
        out_shape=jax.ShapeDtypeStruct((rows, half), F32),
        grid_spec=pltpu.PrefetchScalarGridSpec(
            num_scalar_prefetch=1,
            grid=(1,),
            in_specs=[
                pl.BlockSpec((rows, order), lambda n, pick: (pick[0], 0)),
                fixed((rows, half)),
                fixed((rows, half)),
                fixed((1, order)),
                fixed((1, order)),
            ]
            + [pl.BlockSpec(memory_space=pl.ANY)] * len(after),
            out_specs=fixed((rows, half)),
            scratch_shapes=[pltpu.VMEM((2 * rows, half), BF16)] * 2,
        ),
        compiler_params=pltpu.CompilerParams(vmem_limit_bytes=VMEM_LIMIT),
        cost_estimate=pl.CostEstimate(
            flops=6 * rows * half * half, bytes_accessed=6_000_000, transcendentals=0
        ),
    )(pick, *inputs, *after)


def turn_kernel(count, width, *refs):
    own, got, local_ref, recouple_ref, out_ref, high, low, turned = refs[:2], refs[2:4], *refs[4:]
    half = own[0].shape[1]

    @pl.when(pl.program_id(0) == 0)
    def _():
        for place in range(2):
            span = slice(place * half, (place + 1) * half)
            high[:, span], low[:, span] = split(own[place][...] + got[place][...] - local_ref[:, span])

    turned[...] = dot3(split(recouple_ref[...]), (high[...], low[...]), NT)
    pack(turned, out_ref, count, width)


def turn(own, got, local, recoupling, count, after=()):
    rows, order = local.shape
    width = order // count
    steps = 4
    depth = -(-(rows * width // LANES) // 8) * 8
    return call(
        functools.partial(turn_kernel, count // steps, width),
        jax.ShapeDtypeStruct((count, depth, LANES), F32),
        6 * rows * order * order,
        (*own, *got, local, recoupling),
        [whole(own[0].shape)] * 4
        + [whole(local.shape), pl.BlockSpec((order // steps, order), lambda n: (n, 0))],
        after,
        out_specs=pl.BlockSpec((count // steps, depth, LANES), lambda n: (n, 0, 0)),
        scratch_shapes=[
            pltpu.VMEM((rows, order), BF16),
            pltpu.VMEM((rows, order), BF16),
            pltpu.VMEM((order // steps, rows), F32),
        ],
        grid=(steps,),
    )


def finish_kernel(count, width, where_ref, message_ref, early_ref, late_ref, out_ref, turned):
    rows, order = out_ref.shape
    size, row_index = where_ref[0], where_ref[1]
    cut = early_ref.shape[1]
    unpack(message_ref, turned, count, width)
    for start in range(0, order, TILE):
        span = slice(start, start + TILE)
        ladder = early_ref[:, span] if start < cut else late_ref[:, start - cut : start - cut + TILE]
        total = ladder + turned[span, :].T
        row = lax.broadcasted_iota(jnp.int32, total.shape, 0) + row_index * rows
        column = lax.broadcasted_iota(jnp.int32, total.shape, 1) + start
        out_ref[:, span] = jnp.where((row < size) & (column < size), total, 0.0)


def finish(message, early, late, where):
    rows = early.shape[0]
    order = early.shape[1] + late.shape[1]
    count = message.shape[0]
    return call(
        functools.partial(finish_kernel, count, order // count),
        jax.ShapeDtypeStruct((rows, order), F32),
        FAST,
        (where, message, early, late),
        [SMEM, whole(message.shape), whole(early.shape), whole(late.shape)],
        out_specs=whole((rows, order)),
        scratch_shapes=[pltpu.VMEM((order, rows), F32)],
        grid=(1,),
    )


def hold_kernel(x_ref, out_ref):
    del x_ref, out_ref


def hold(x, *after):
    return call(
        hold_kernel,
        jax.ShapeDtypeStruct(x.shape, x.dtype),
        FAST,
        (x,),
        [pl.BlockSpec(memory_space=pl.ANY)],
        after,
        out_specs=pl.BlockSpec(memory_space=pl.ANY),
        input_output_aliases={0: 0},
    )


def exchange(message):
    return lax.all_to_all(message, "chan", 0, 0, tiled=True)


def reduced(part):
    return lax.psum_scatter(part, "row", scatter_dimension=0, tiled=True)


def shards(generator, hamiltonian, recoupling, channel_size, hole_first, hole_second):
    gen, ham, recouple = generator[0], hamiltonian[0], recoupling[0]
    rows = gen.shape[0]
    half = gen.shape[1] // 2
    count = lax.axis_size("chan")
    holes = (hole_first, hole_second)
    row = lax.axis_index("row").astype(jnp.int32)
    where = jnp.stack([channel_size[0], row])
    near, far = row ^ 1, 3 - row
    is_outer = (row == 0) | (row == 3)
    far_own = jnp.where(row < 2, 0, rows)
    near_own = jnp.where(row % 2 == 0, 0, rows)
    far_kind = jnp.where(is_outer, 0, 1)
    near_kind = jnp.where(row < 2, 2, 3)

    def pick(block, own, kind):
        return jnp.stack([block, own, kind]).astype(jnp.int32)

    def to_near(x):
        return lax.ppermute(x, "row", [(0, 1), (1, 0), (2, 3), (3, 2)])

    def to_far(x):
        return lax.ppermute(x, "row", [(0, 3), (3, 0), (1, 2), (2, 1)])

    gen_message = encode(gen, where, count)
    gen_moved = exchange(gen_message)
    early_part, late_part = ladder_part(gen, ham, *holes, where, after=(gen_message,))
    early = reduced(early_part)
    ham_message = encode(ham, where, count, after=(early_part,))
    gen_bar = bar(gen_moved, recouple, rows, False, after=(ham_message,))
    gen_all = lax.all_gather(hold(gen_bar, early), "row", axis=0, tiled=True)
    ham_moved = exchange(hold(ham_message, gen_bar))
    ham_bar = bar(ham_moved, recouple, rows, True)
    from_far = to_far(ham_bar[0])
    from_near = to_near(ham_bar[1])
    local = local_term(gen_all, ham_bar, *holes)
    send_near = pair_product(pick(near, far_own, far_kind), gen_all, ham_bar[0], from_far, *holes, after=(local,))
    got_near = to_near(send_near)
    send_far = pair_product(pick(far, near_own, near_kind), gen_all, ham_bar[1], from_near, *holes, after=(local,))
    got_far = to_far(send_far)
    own = (
        pair_product(pick(row, far_own, far_kind), gen_all, ham_bar[0], from_far, *holes, after=(send_near, send_far)),
        pair_product(pick(row, near_own, near_kind), gen_all, ham_bar[1], from_near, *holes, after=(send_near, send_far)),
    )
    message = turn(own, (got_near, got_far), local, recouple, count)
    back = exchange(message)
    late = reduced(hold(late_part, message))
    return finish(back, early, late, where)[None]


def solution(mesh):
    in_specs = (
        P("chan", "row", None),
        P("chan", "row", None),
        P("chan", None, None),
        P("chan"),
        P("chan", None),
        P("chan", None),
    )
    out_specs = P("chan", "row", None)
    return jax.shard_map(shards, mesh=mesh, in_specs=in_specs, out_specs=out_specs, check_vma=False)
```

time: 316 us -> 305 us (0.965)
  waiting for transfers between devices: 102 us -> 60 us
  Pallas kernels: 77.6 us -> 97.5 us
  starting transfers between devices: 10.8 us -> 16.6 us
  local copies, waits for them, and re-layouts: 1.25 us -> 6.22 us
    all_gather x2 -> x1, waiting for transfers between devices: 56.7 us -> 3.97 us  [shards(): gen_all = lax.all_gather(hold(gen_bar, early), 'row', axis=0, tiled=True)]
    reduce_scatter x1 -> x2, waiting for transfers between devices: 38.1 us -> 0.02 us  [reduced(): return lax.psum_scatter(part, 'row', scatter_dimension=0, tiled=True)]
    all_to_all x1, waiting for transfers between devices: 7.5 us -> 39.8 us  [exchange(): return lax.all_to_all(message, 'chan', 0, 0, tiled=True)]
    pallas_call x8 -> x15, Pallas kernels: 77.6 us -> 97.5 us  [the longest x11 75.7 us: call(): pl.pallas_call(body, out_shape=out_shape, in_specs=list(in_specs) + [pl.B...]
    ppermute x0 -> x4, waiting for transfers between devices: none -> 15.4 us  [the longest x2 15.1 us: to_far(): return lax.ppermute(x, 'row', [(0, 3), (3, 0), (1, 2), (2, 1)])]
    unnamed x2 -> x14, local copies, waits for them, and re-layouts: 1.25 us -> 6.22 us
    ppermute x0 -> x4, starting transfers between devices: none -> 4.44 us  [the longest x2 2.97 us: to_far(): return lax.ppermute(x, 'row', [(0, 3), (3, 0), (1, 2), (2, 1)])]
  transfers between devices with their start and end apart: 4 -> 8, of which waited for: 3 -> 5; matrix products, arithmetic and copies ran while one was open for 0% -> 1% of each run, Pallas kernels for 17% -> 19%
where the time goes in v2:
time: 305 us; the launch traced here: 304 us
  blocking collectives  108 us (35%)
  Pallas kernels  97.5 us (32%)
  waiting for transfers between devices  60 us (20%)
  starting transfers between devices  16.6 us (5%)
  between operations  13.8 us (5%)
  local copies, waits for them, and re-layouts  6.22 us (2%)
    all_to_all x2, blocking collectives, exchange(): return lax.all_to_all(message, 'chan', 0, 0, tiled=True)  108 us
    pallas_call x11, Pallas kernels, call(): pl.pallas_call(body, out_shape=out_shape, in_specs=list(in_specs) + [pl.B...  75.7 us
    all_to_all x1, waiting for transfers between devices, exchange(): return lax.all_to_all(message, 'chan', 0, 0, tiled=True)  39.8 us
    pallas_call x4, Pallas kernels, pair_product(): pl.pallas_call(body, out_shape=jax.ShapeDtypeStruct((rows, half), F32), g...  21.7 us
    ppermute x2, waiting for transfers between devices, to_far(): return lax.ppermute(x, 'row', [(0, 3), (3, 0), (1, 2), (2, 1)])  15.1 us
    all_to_all x1, starting transfers between devices, exchange(): return lax.all_to_all(message, 'chan', 0, 0, tiled=True)  12.1 us
    unnamed x14, local copies, waits for them, and re-layouts  6.22 us
  transfers between devices with their start and end apart: 8, of which 5 were waited for; matrix products, arithmetic and copies ran while one was open for 1% of the time, Pallas kernels for 19%

profile of v2, /device:TPU:8, one launch (start us, length us, event | category | flops | bytes accessed | tf_op | source)
XLA Modules:
  0.0 304.4 jit_solution(18201867394270610928)
XLA Ops:
  7.2 0.7 pad_add_fusion.refs_0_
  7.9 5.8 %shard_map.64.refs_5_ = f32[64,56,128]{2,1,0:T(8,128)} custom-call(s32[2]{0:T(128)} %pad_add_fusion.refs_0_, f32[320,1280]{1,0:T(8,128)} %bitcast.14), custom_call_target="tpu_custom_call" | custom-call | flops 1000 | bytes 8000000 | tf_op jit(solution)/shard_map/pallas_call | solution.py:38
  13.6 15.7 %shard_map.65 = (f32[1280,512]{1,0:T(8,128)}, f32[1280,768]{1,0:T(8,128)}) custom-call(s32[2]{0:T(128)} %pad_add_fusion.refs_0_, f32[320,1280]{1,0:T(8,128)} %bitcast.15, f32[320,1280]{1,0:T(8,128)} %bitcast.16, s32[1,1280]{1,0:T(1,128)} %refs_4_.11, s32[1,1280]{1,0:T(1,128)} %refs_5_.7, f32[64,56,128]{2,1,0:T(8,128)} %shard_map.64.refs_5_), custom_call_target="tpu_custom_call" | custom-call | flops 6291456000 | bytes 8000000 | tf_op jit(solution)/shard_map/pallas_call | solution.py:38
  29.4 12.1 %all-to-all-start = ((f32[64,56,128]{2,1,0:T(8,128)}), f32[64,56,128]{2,1,0:T(8,128)S(1)}, u32[]{:S(2)}, u32[]{:S(2)}) async-start(f32[64,56,128]{2,1,0:T(8,128)} %shard_map.64.refs_5_), calls=%async_computation | async-start | bytes 3670016 | tf_op jit(solution)/shard_map/all_to_all | solution.py:405
  41.5 5.8 %shard_map.66.refs_2_.refs_0_ = f32[64,56,128]{2,1,0:T(8,128)} custom-call(s32[2]{0:T(128)} %pad_add_fusion.refs_0_, f32[320,1280]{1,0:T(8,128)} %bitcast.17, f32[1280,512]{1,0:T(8,128)} %get-tuple-element.9.refs_2_), custom_call_target="tpu_custom_call" | custom-call | flops 1000 | bytes 8000000 | tf_op jit(solution)/shard_map/pallas_call | solution.py:38
  47.3 39.8 %all-to-all-done.refs_0_ = f32[64,56,128]{2,1,0:T(8,128)S(1)} async-done(((f32[64,56,128]{2,1,0:T(8,128)}), f32[64,56,128]{2,1,0:T(8,128)S(1)}, u32[]{:S(2)}, u32[]{:S(2)}) %all-to-all-start) | async-done | bytes 1835040 | tf_op jit(solution)/shard_map/all_to_all | solution.py:405
  87.1 1.3 copy-done.2
  88.4 10.9 %shard_map.67.refs_0_.refs_1_ = f32[320,1280]{1,0:T(8,128)} custom-call(f32[64,56,128]{2,1,0:T(8,128)} %copy-done.2, f32[1280,1280]{1,0:T(8,128)} %bitcast.11, f32[64,56,128]{2,1,0:T(8,128)} %shard_map.66.refs_2_.refs_0_), custom_call_target="tpu_custom_call" | custom-call | flops 3145728000 | bytes 8000000 | tf_op jit(solution)/shard_map/pallas_call | solution.py:38
  99.4 0.7 all-gather.2.cloned.1.call-update
  100.1 0.7 copy-done
  100.9 51.0 %all_to_all.15.refs_0_ = f32[64,56,128]{2,1,0:T(8,128)} all-to-all(f32[64,56,128]{2,1,0:T(8,128)S(1)} %copy-done), channel_id=1, replica_groups=mesh['chan'=64,'row'=4] {'chan'}, dimensions={0} | all-to-all | bytes 3670016 | tf_op jit(solution)/shard_map/all_to_all | solution.py:405
  151.8 11.0 %shard_map.70 = (f32[320,640]{1,0:T(8,128)}, f32[320,640]{1,0:T(8,128)}) custom-call(f32[64,56,128]{2,1,0:T(8,128)} %all_to_all.15.refs_0_, f32[1280,1280]{1,0:T(8,128)} %bitcast.12), custom_call_target="tpu_custom_call" | custom-call | flops 3145728000 | bytes 8000000 | tf_op jit(solution)/shard_map/pallas_call | solution.py:38
  162.8 2.7 collective-permute-start
  165.8 0.7 add_add_fusion.1.refs_0_
  166.4 0.6 add_add_fusion.2.refs_0_
  167.0 4.0 %all-gather.2.cloned.1.call-done.refs_0_.refs_1_ = f32[1280,1280]{1,0:T(8,128)} async-done(((f32[320,1280]{1,0:T(8,128)}), f32[1280,1280]{1,0:T(8,128)}) %all-gather.2.cloned.1.call-update) | async-done | bytes 6553616 | tf_op jit(solution)/shard_map/all_gather | solution.py:442
  171.0 8.2 %shard_map.71.refs_6_.refs_4_ = f32[320,1280]{1,0:T(8,128)} custom-call(f32[1280,1280]{1,0:T(8,128)} %all-gather.2.cloned.1.call-done.refs_0_.refs_1_, f32[320,640]{1,0:T(8,128)} %get-tuple-element.10.refs_1_.refs_2_, f32[320,640]{1,0:T(8,128)} %get-tuple-element.11.refs_2_, s32[1,1280]{1,0:T(1,128)} %refs_4_.11, s32[1,1280]{1,0:T(1,128)} %refs_5_.7), custom_call_target="tpu_custom_call" | custom-call | flops 3145728000 | bytes 8000000 | tf_op jit(solution)/shard_map/pallas_call | solution.py:38
  179.2 6.6 %collective-permute-done.refs_3_ = f32[320,640]{1,0:T(8,128)S(1)} collective-permute-done((f32[320,640]{1,0:T(8,128)}, f32[320,640]{1,0:T(8,128)S(1)}, u32[]{:S(2)}, u32[]{:S(2)}) %collective-permute-start) | collective-permute-done | bytes 819232 | tf_op jit(solution)/shard_map/ppermute | solution.py:434
  185.8 0.9 copy-done.3
  186.7 5.5 %shard_map.72.refs_6_ = f32[320,640]{1,0:T(8,128)} custom-call(s32[3]{0:T(128)} %add_add_fusion.1.refs_0_, f32[1280,1280]{1,0:T(8,128)} %all-gather.2.cloned.1.call-done.refs_0_.refs_1_, f32[320,640]{1,0:T(8,128)} %get-tuple-element.10.refs_1_.refs_2_, f32[320,640]{1,0:T(8,128)} %copy-done.3, s32[1,1280]{1,0:T(1,128)} %refs_4_.11, s32[1,1280]{1,0:T(1,128)} %refs_5_.7, ...), custom_call_target="tpu_custom_call" | custom-call | flops 786432000 | bytes 6000000 | tf_op jit(solution)/shard_map/pallas_call | solution.py:296
  192.2 1.2 collective-permute-start.2
  193.4 0.9 copy-done.4
  194.3 5.4 %shard_map.73.refs_7_ = f32[320,640]{1,0:T(8,128)} custom-call(s32[3]{0:T(128)} %add_add_fusion.2.refs_0_, f32[1280,1280]{1,0:T(8,128)} %all-gather.2.cloned.1.call-done.refs_0_.refs_1_, f32[320,640]{1,0:T(8,128)} %get-tuple-element.11.refs_2_, f32[320,640]{1,0:T(8,128)} %copy-done.4, s32[1,1280]{1,0:T(1,128)} %refs_4_.11, s32[1,1280]{1,0:T(1,128)} %refs_5_.7, ...), custom_call_target="tpu_custom_call" | custom-call | flops 786432000 | bytes 6000000 | tf_op jit(solution)/shard_map/pallas_call | solution.py:296
  200.0 0.6 add_add_fusion
  200.6 5.4 %shard_map.75.refs_1_ = f32[320,640]{1,0:T(8,128)} custom-call(s32[3]{0:T(128)} %get-tuple-element.14.refs_0_, f32[1280,1280]{1,0:T(8,128)} %all-gather.2.cloned.1.call-done.refs_0_.refs_1_, f32[320,640]{1,0:T(8,128)} %get-tuple-element.11.refs_2_, f32[320,640]{1,0:T(8,128)} %copy-done.4, s32[1,1280]{1,0:T(1,128)} %refs_4_.11, s32[1,1280]{1,0:T(1,128)} %refs_5_.7, ...), custom_call_target="tpu_custom_call" | custom-call | flops 786432000 | bytes 6000000 | tf_op jit(solution)/shard_map/pallas_call | solution.py:296
  206.1 5.4 %shard_map.74.refs_0_ = f32[320,640]{1,0:T(8,128)} custom-call(s32[3]{0:T(128)} %get-tuple-element.13.refs_0_, f32[1280,1280]{1,0:T(8,128)} %all-gather.2.cloned.1.call-done.refs_0_.refs_1_, f32[320,640]{1,0:T(8,128)} %get-tuple-element.10.refs_1_.refs_2_, f32[320,640]{1,0:T(8,128)} %copy-done.3, s32[1,1280]{1,0:T(1,128)} %refs_4_.11, s32[1,1280]{1,0:T(1,128)} %refs_5_.7, ...), custom_call_target="tpu_custom_call" | custom-call | flops 786432000 | bytes 6000000 | tf_op jit(solution)/shard_map/pallas_call | solution.py:296
  211.8 8.5 %collective-permute-done.3.refs_3_ = f32[320,640]{1,0:T(8,128)S(1)} collective-permute-done((f32[320,640]{1,0:T(8,128)}, f32[320,640]{1,0:T(8,128)S(1)}, u32[]{:S(2)}, u32[]{:S(2)}) %collective-permute-start.3) | collective-permute-done | bytes 819232 | tf_op jit(solution)/shard_map/ppermute | solution.py:434
  220.3 0.9 copy-done.6
  221.2 12.2 %shard_map.76.refs_1_ = f32[64,56,128]{2,1,0:T(8,128)} custom-call(f32[320,640]{1,0:T(8,128)} %shard_map.74.refs_0_, f32[320,640]{1,0:T(8,128)} %shard_map.75.refs_1_, f32[320,640]{1,0:T(8,128)} %copy-done.5, f32[320,640]{1,0:T(8,128)} %copy-done.6, f32[320,1280]{1,0:T(8,128)} %shard_map.71.refs_6_.refs_4_, f32[1280,1280]{1,0:T(8,128)} %bitcast.13), custom_call_target="tpu_custom_call" | custom-call | flops 3145728000 | bytes 8000000 | tf_op jit(solution)/shard_map/pallas_call | solution.py:38
  233.5 1.5 copy-done.1
  235.0 56.9 %all_to_all.16.refs_1_ = f32[64,56,128]{2,1,0:T(8,128)} all-to-all(f32[64,56,128]{2,1,0:T(8,128)S(1)} %copy-done.1), channel_id=1, replica_groups=mesh['chan'=64,'row'=4] {'chan'}, dimensions={0} | all-to-all | bytes 3670016 | tf_op jit(solution)/shard_map/all_to_all | solution.py:405
  291.8 6.1 %shard_map.78 = f32[320,1280]{1,0:T(8,128)} custom-call(s32[2]{0:T(128)} %pad_add_fusion.refs_0_, f32[64,56,128]{2,1,0:T(8,128)} %all_to_all.16.refs_1_, f32[320,512]{1,0:T(8,128)} %reduce-scatter.3.cloned.1.call-done.refs_1_.refs_2_, f32[320,768]{1,0:T(8,128)} %reduce-scatter.5.cloned.1.call-done.refs_3_), custom_call_target="tpu_custom_call" | custom-call | flops 1000 | bytes 8000000 | tf_op jit(solution)/shard_map/pallas_call | solution.py:38
  (22 shorter events, 1.0 us)
Async XLA Ops:
  6.5 92.8 %reduce-scatter.3.cloned.1.call-start = ((), (), s32[]{:S(2)}) async-start(), calls=%async_computation.5 | async-start | bytes 3276800 | tf_op jit(solution)/shard_map/reduce_scatter | solution.py:409
  29.4 57.8 %all-to-all-start = ((f32[64,56,128]{2,1,0:T(8,128)}), f32[64,56,128]{2,1,0:T(8,128)S(1)}, u32[]{:S(2)}, u32[]{:S(2)}) async-start(f32[64,56,128]{2,1,0:T(8,128)} %shard_map.64.refs_5_), calls=%async_computation | async-start | bytes 3670016 | tf_op jit(solution)/shard_map/all_to_all | solution.py:405
  87.1 1.3 copy-start.2
  99.4 1.5 copy-start
  99.4 71.6 %all-gather.2.cloned.1.call-start = ((), (), s32[]{:S(2)}) async-start(), calls=%async_computation.6 | async-start | bytes 8192000 | tf_op jit(solution)/shard_map/all_gather | solution.py:442
  100.1 191.7 %reduce-scatter.5.cloned.1.call-start = ((), (), s32[]{:S(2)}) async-start(), calls=%async_computation.7 | async-start | bytes 4915200 | tf_op jit(solution)/shard_map/reduce_scatter | solution.py:409
  162.8 23.0 %collective-permute-start = (f32[320,640]{1,0:T(8,128)}, f32[320,640]{1,0:T(8,128)S(1)}, u32[]{:S(2)}, u32[]{:S(2)}) collective-permute-start(f32[320,640]{1,0:T(8,128)} %get-tuple-element.10.refs_1_.refs_2_), channel_id=1, source_target_pairs={{0,3},{3,0},{1,2},{2,1},{4,7},{7,4},{5,6},{6,5},{8,11},{11,8},{9,1... | collective-permute-start | bytes 2457608 | tf_op jit(solution)/shard_map/ppermute | solution.py:434
  165.5 27.9 %collective-permute-start.1 = (f32[320,640]{1,0:T(8,128)}, f32[320,640]{1,0:T(8,128)S(1)}, u32[]{:S(2)}, u32[]{:S(2)}) collective-permute-start(f32[320,640]{1,0:T(8,128)} %get-tuple-element.11.refs_2_), channel_id=1, source_target_pairs={{0,1},{1,0},{2,3},{3,2},{4,5},{5,4},{6,7},{7,6},{8,9},{9,8},{10,11... | collective-permute-start | bytes 2457608 | tf_op jit(solution)/shard_map/ppermute | solution.py:431
  185.8 0.9 copy-start.3
  192.2 19.7 %collective-permute-start.2 = (f32[320,640]{1,0:T(8,128)}, f32[320,640]{1,0:T(8,128)S(1)}, u32[]{:S(2)}, u32[]{:S(2)}) collective-permute-start(f32[320,640]{1,0:T(8,128)} %shard_map.72.refs_6_), channel_id=1, source_target_pairs={{0,1},{1,0},{2,3},{3,2},{4,5},{5,4},{6,7},{7,6},{8,9},{9,8},{10,11... | collective-permute-start | bytes 2457608 | tf_op jit(solution)/shard_map/ppermute | solution.py:431
  193.4 0.9 copy-start.4
  199.7 20.6 %collective-permute-start.3 = (f32[320,640]{1,0:T(8,128)}, f32[320,640]{1,0:T(8,128)S(1)}, u32[]{:S(2)}, u32[]{:S(2)}) collective-permute-start(f32[320,640]{1,0:T(8,128)} %shard_map.73.refs_7_), channel_id=1, source_target_pairs={{0,3},{3,0},{1,2},{2,1},{4,7},{7,4},{5,6},{6,5},{8,11},{11,8},{9,1... | collective-permute-start | bytes 2457608 | tf_op jit(solution)/shard_map/ppermute | solution.py:434
  211.8 8.5 %copy-start.5 = (f32[320,640]{1,0:T(8,128)}, f32[320,640]{1,0:T(8,128)S(1)}, u32[]{:S(2)}) copy-start(f32[320,640]{1,0:T(8,128)S(1)} %collective-permute-done.2.refs_2_) | copy-start | bytes 2457604
  220.3 0.9 copy-start.6
  233.5 1.5 copy-start.1
Sparse Core Ops, SparseCore 0:
  29.5 39.3 reduce-scatter.2
  102.0 68.9 all-gather.1
  233.6 46.8 reduce-scatter.4

commit v3 on v0

v3 whole, which is shorter than its diff:
```python
import functools

import jax
import jax.numpy as jnp
from jax import lax
from jax.experimental import pallas as pl
from jax.experimental.pallas import tpu as pltpu
from jax.sharding import PartitionSpec as P

F32 = jnp.float32
BF16 = jnp.bfloat16
MIB = 1024 * 1024
LARGE = 62
NN = ((1,), (0,))
NT = ((1,), (1,))
TILE = 256
LANES = 128
SUB = 8
FAST = 1000
SLOW = 10**12


def split(x):
    high = x.astype(BF16)
    return high, (x - high.astype(F32)).astype(BF16)


def dot3(a, b, dims):
    def one(left, right):
        return lax.dot_general(left, right, (dims, ((), ())), preferred_element_type=F32)

    return one(a[0], b[0]) + (one(a[0], b[1]) + one(a[1], b[0]))


VMEM = pl.BlockSpec(memory_space=pltpu.VMEM)
SMEM = pl.BlockSpec(memory_space=pltpu.SMEM)
ANY = pl.BlockSpec(memory_space=pl.ANY)


def call(kernel, out_shape, mib, inputs, after=(), flops=FAST, in_specs=None, out_specs=None, scratch_shapes=(), aliases=None):
    first, last = len(inputs), len(inputs) + len(after)

    def body(*refs):
        kernel(*refs[:first], *refs[last:])

    if in_specs is None:
        in_specs = [SMEM if x.ndim == 1 else VMEM for x in inputs]
    if out_specs is None:
        out_specs = [VMEM] * len(out_shape) if isinstance(out_shape, list) else VMEM
    return pl.pallas_call(
        body,
        out_shape=out_shape,
        in_specs=list(in_specs) + [ANY] * len(after),
        out_specs=out_specs,
        scratch_shapes=list(scratch_shapes),
        input_output_aliases=aliases or {},
        compiler_params=pltpu.CompilerParams(vmem_limit_bytes=mib * MIB),
        cost_estimate=pl.CostEstimate(flops=flops, bytes_accessed=4_000_000, transcendentals=0),
    )(*inputs, *after)


def message_shape(rows, order, count):
    return jax.ShapeDtypeStruct((count, 1, rows * order // count), F32)


def upper(shape):
    return lax.broadcasted_iota(jnp.int32, shape, 0) < shape[0] // 2


def swapped(x):
    middle = x.shape[0] // 2
    return jnp.concatenate([x[middle:], x[:middle]], axis=0)


def put(target, channel, at, tile):
    target[channel, :, at : at + tile.size] = tile.reshape(1, tile.size)
    return at + tile.size


def get(source, channel, at, rows):
    return source[channel, :, at : at + rows * LANES].reshape(rows, LANES)


def lane_parts(rows):
    return [(lane, min(LANES, rows - lane)) for lane in range(0, rows, LANES)]


def pack(source, target, count, width):
    parts = lane_parts(source.shape[1])

    def pair(step, _):
        base = pl.multiple_of(step * 2 * width, SUB)
        whole = ([], [])
        last = ([], [])
        for lane, size in parts:
            tile = [source[pl.ds(base + SUB * k, SUB), lane : lane + size] for k in range(5)]
            top = upper(tile[0].shape)
            turned = [swapped(tile[k]) for k in range(2, 5)]
            whole[0].append(tile[:2])
            last[0].append(tile[2])
            whole[1].append([jnp.where(top, turned[0], turned[1]), jnp.where(top, turned[1], turned[2])])
            last[1].append(turned[2])
        top = upper((SUB, LANES))
        for odd in range(2):
            channel = 2 * step + odd
            at = 0
            for tiles in whole[odd][:-1]:
                for tile in tiles:
                    at = put(target, channel, at, tile)
            at = put(target, channel, at, jnp.concatenate(whole[odd][-1], axis=1))
            first, second, tail = last[odd]
            at = put(target, channel, at, jnp.where(top, first, swapped(second)))
            put(target, channel, at, jnp.concatenate([tail[: SUB // 4], tail[SUB // 4 : SUB // 2]], axis=1))
        return 0

    lax.fori_loop(0, count // 2, pair, 0, unroll=4)


def unpack(source, target, count, width):
    parts = lane_parts(target.shape[1])
    rest = parts[-1][1]
    size = SUB * LANES

    def pair(step, _):
        base = pl.multiple_of(step * 2 * width, SUB)
        whole = ([], [])
        last = ([], [])
        for odd in range(2):
            channel = 2 * step + odd
            at = 0
            for _ in parts[:-1]:
                whole[odd].append([get(source, channel, at, SUB), get(source, channel, at + size, SUB)])
                at += 2 * size
            tail = get(source, channel, at, SUB)
            whole[odd].append([tail[:, :rest], tail[:, rest:]])
            at += size
            shared = get(source, channel, at, SUB)
            corner = get(source, channel, at + size, SUB // 4)
            corner = [corner[:, :rest], corner[:, rest:]]
            last[odd].extend([shared, swapped(shared), jnp.concatenate(corner + corner, axis=0)])
        for place, (lane, size_) in enumerate(parts):
            even, odd = whole[0][place], [swapped(tile) for tile in whole[1][place]]
            top = upper(even[0].shape)
            tiles = even + [
                jnp.where(top, last[0][place], odd[0]),
                jnp.where(top, odd[0], odd[1]),
                jnp.where(top, odd[1], swapped(last[1][place])),
            ]
            for k, tile in enumerate(tiles):
                target[pl.ds(base + SUB * k, SUB), lane : lane + size_] = tile
        return 0

    lax.fori_loop(0, count // 2, pair, 0, unroll=4)


def live(shape, where_ref, rows, start):
    row = lax.broadcasted_iota(jnp.int32, shape, 0) + where_ref[1] * rows
    column = lax.broadcasted_iota(jnp.int32, shape, 1) + start
    return (row < where_ref[0]) & (column < where_ref[0])


def encode_kernel(count, where_ref, x_ref, out_ref, turned):
    rows, order = x_ref.shape
    for start in range(0, order, TILE):
        block = x_ref[:, start : start + TILE]
        turned[start : start + TILE, :] = jnp.where(live(block.shape, where_ref, rows, start), block, 0.0).T
    pack(turned, out_ref, count, order // count)


def encode(x, where, count, after=()):
    rows, order = x.shape
    return call(
        functools.partial(encode_kernel, count),
        message_shape(rows, order, count),
        12,
        (where, x),
        after,
        scratch_shapes=[pltpu.VMEM((order, rows), F32)],
    )


def read_kernel(message_ref, high, low, turned):
    order = turned.shape[0]
    count = message_ref.shape[0]
    unpack(message_ref, turned, count, order // count)
    for start in range(0, order, TILE):
        span = slice(start, start + TILE)
        high[:, span], low[:, span] = split(turned[span, :].T)


def read(message, rows, after=(), flops=FAST):
    order = message.shape[0] * message.shape[2] // rows
    return call(
        read_kernel,
        [jax.ShapeDtypeStruct((rows, order), BF16)] * 2,
        12,
        (message,),
        after,
        flops,
        scratch_shapes=[pltpu.VMEM((order, rows), F32)],
    )


def bar_kernel(high, low, recouple_ref, *outs):
    order = recouple_ref.shape[0]
    width = order // len(outs)
    for start in range(0, order, TILE):
        product = dot3((high[...], low[...]), split(recouple_ref[:, start : start + TILE]), NN)
        for place, out in enumerate(outs):
            begin, end = max(start, place * width), min(start + TILE, (place + 1) * width)
            if begin < end:
                out[:, begin - place * width : end - place * width] = product[:, begin - start : end - start]


def bar(moved, recoupling, parts, flops=FAST):
    rows, order = moved[0].shape
    return call(
        bar_kernel,
        [jax.ShapeDtypeStruct((rows, order // parts), F32)] * parts,
        20,
        (*moved, recoupling),
        flops=flops,
    )


def ladder_kernel(where_ref, gen_ref, ham_ref, first_ref, second_ref, early_ref, late_ref, left_high, left_low, right_high, right_low):
    rows, order = gen_ref.shape
    cut = early_ref.shape[1]
    position = lax.broadcasted_iota(jnp.int32, (1, order), 1)
    weight = jnp.where(position < where_ref[0], (first_ref[...] + second_ref[...] - 1).astype(F32), 0.0)
    mine = weight[:, :rows]
    for other in range(1, order // rows):
        mine = jnp.where(where_ref[1] == other, weight[:, other * rows : (other + 1) * rows], mine)
    for place, (left, right) in enumerate(((gen_ref, ham_ref), (ham_ref, gen_ref))):
        span = slice(place * rows, (place + 1) * rows)
        for start in range(0, order, TILE):
            piece = split(left[:, start : start + TILE].T * mine)
            left_high[start : start + TILE, span] = piece[0]
            left_low[start : start + TILE, span] = piece[1]
        right_high[span, :], right_low[span, :] = split(right[...])
    for start in range(0, order, TILE):
        columns = slice(start, start + TILE)
        right = right_high[:, columns], right_low[:, columns]
        out, at = (early_ref, start) if start < cut else (late_ref, start - cut)
        out[:, at : at + TILE] = dot3((left_high[...], left_low[...]), right, NN)


def ladder_part(gen, ham, first, second, where, after=()):
    rows, order = gen.shape
    cut = order // TILE // 2 * TILE
    return call(
        ladder_kernel,
        [jax.ShapeDtypeStruct((order, cut), F32), jax.ShapeDtypeStruct((order, order - cut), F32)],
        28,
        (where, gen, ham, first, second),
        after,
        scratch_shapes=[pltpu.VMEM((order, 2 * rows), BF16)] * 2 + [pltpu.VMEM((2 * rows, order), BF16)] * 2,
    )


def weighted(first_ref, second_ref):
    return (first_ref[...] - second_ref[...]).astype(F32)


def local_kernel(gen_all, low_ref, high_ref, first_ref, second_ref, out_ref, ham_high, ham_low):
    half = low_ref.shape[1]
    weight = weighted(first_ref, second_ref)
    for place, ref in enumerate((low_ref, high_ref)):
        span = slice(place * half, (place + 1) * half)
        ham_high[:, span], ham_low[:, span] = split(ref[...] * weight[:, span])
    for start in range(0, 2 * half, TILE):
        span = slice(start, start + TILE)
        out_ref[:, span] = dot3((ham_high[...], ham_low[...]), split(gen_all[:, span]), NN)


def local_term(gen_all, ham_halves, first, second, after=()):
    rows, half = ham_halves[0].shape
    return call(
        local_kernel,
        jax.ShapeDtypeStruct((rows, 2 * half), F32),
        16,
        (gen_all, *ham_halves, first, second),
        after,
        scratch_shapes=[pltpu.VMEM((rows, 2 * half), BF16)] * 2,
    )


def pair_kernel(pick_ref, gen_all, own_ref, got_ref, first_ref, second_ref, out_ref, right_high, right_low):
    rows, half = own_ref.shape
    order = 2 * half
    kind = pick_ref[2]
    scaled = gen_all[pl.ds(pl.multiple_of(pick_ref[0] * rows, 64), rows), :] * weighted(first_ref, second_ref)
    outer = jnp.concatenate([scaled[:, :rows], scaled[:, order - rows :]], axis=1)
    inner = scaled[:, rows : order - rows]
    ends = jnp.where(kind == 2, scaled[:, :half], scaled[:, half:])
    left = split(jnp.where(kind == 0, outer, jnp.where(kind == 1, inner, ends)))
    own_at = pl.multiple_of(pick_ref[1], 64)
    got_at = pl.multiple_of(rows - pick_ref[1], 64)
    for at, ref in ((own_at, own_ref), (got_at, got_ref)):
        right_high[pl.ds(at, rows), :], right_low[pl.ds(at, rows), :] = split(ref[...])
    out_ref[...] = dot3(left, (right_high[...], right_low[...]), NN)


def pair_product(pick, gen_all, own, got, first, second, after=()):
    rows, half = own.shape
    return call(
        pair_kernel,
        jax.ShapeDtypeStruct((rows, half), F32),
        20,
        (pick, gen_all, own, got, first, second),
        after,
        scratch_shapes=[pltpu.VMEM((2 * rows, half), BF16)] * 2,
    )


def turn_kernel(count, *refs):
    own, got, local_ref, recouple_ref, out_ref, token_ref, high, low, turned = refs[:2], refs[2:4], *refs[4:]
    token_ref[...] = jnp.zeros_like(token_ref)
    half = own[0].shape[1]
    for place in range(2):
        span = slice(place * half, (place + 1) * half)
        high[:, span], low[:, span] = split(own[place][...] + got[place][...] - local_ref[:, span])
    order = recouple_ref.shape[0]
    for start in range(0, order, TILE):
        span = slice(start, start + TILE)
        turned[span, :] = dot3((high[...], low[...]), split(recouple_ref[span, :]), NT).T
    pack(turned, out_ref, count, order // count)


def turn(own, got, local, recoupling, count, after=()):
    rows, order = local.shape
    return call(
        functools.partial(turn_kernel, count),
        [message_shape(rows, order, count), jax.ShapeDtypeStruct((SUB, LANES), F32)],
        24,
        (*own, *got, local, recoupling),
        after,
        scratch_shapes=[
            pltpu.VMEM((rows, order), BF16),
            pltpu.VMEM((rows, order), BF16),
            pltpu.VMEM((order, rows), F32),
        ],
    )


def finish_kernel(where_ref, message_ref, early_hbm, late_hbm, out_ref, turned, ladder_ref, arrived):
    rows, order = out_ref.shape
    cut = early_hbm.shape[1]
    count = message_ref.shape[0]
    copies = [
        pltpu.make_async_copy(early_hbm, ladder_ref.at[:, pl.ds(0, cut)], arrived.at[0]),
        pltpu.make_async_copy(late_hbm, ladder_ref.at[:, pl.ds(cut, order - cut)], arrived.at[1]),
    ]
    for copy in copies:
        copy.start()
    unpack(message_ref, turned, count, order // count)
    for copy in copies:
        copy.wait()
    for start in range(0, order, TILE):
        span = slice(start, start + TILE)
        total = ladder_ref[:, span] + turned[span, :].T
        out_ref[:, span] = jnp.where(live(total.shape, where_ref, rows, start), total, 0.0)


def finish(message, early, late, where):
    rows = early.shape[0]
    order = early.shape[1] + late.shape[1]
    return call(
        finish_kernel,
        jax.ShapeDtypeStruct((rows, order), F32),
        LARGE,
        (where, message, early, late),
        in_specs=[SMEM, VMEM, ANY, ANY],
        scratch_shapes=[
            pltpu.VMEM((order, rows), F32),
            pltpu.VMEM((rows, order), F32),
            pltpu.SemaphoreType.DMA((2,)),
        ],
    )


def hold_kernel(x_ref, out_ref):
    del x_ref, out_ref


def hold(x, after, mib):
    return call(
        hold_kernel,
        jax.ShapeDtypeStruct(x.shape, x.dtype),
        mib,
        (x,),
        (after,),
        in_specs=[ANY],
        out_specs=ANY,
        aliases={0: 0},
    )


def exchange(message):
    return lax.all_to_all(message, "chan", 0, 0, tiled=True)


def reduced(part):
    return lax.psum_scatter(part, "row", scatter_dimension=0, tiled=True)


def shards(generator, hamiltonian, recoupling, channel_size, hole_first, hole_second):
    gen, ham, recouple = generator[0], hamiltonian[0], recoupling[0]
    rows = gen.shape[0]
    count = lax.axis_size("chan")
    holes = (hole_first, hole_second)
    row = lax.axis_index("row").astype(jnp.int32)
    where = jnp.stack([channel_size[0], row])
    far_own, far_kind = jnp.where(row < 2, 0, rows), jnp.where((row == 0) | (row == 3), 0, 1)
    near_own, near_kind = jnp.where(row % 2 == 0, 0, rows), jnp.where(row < 2, 2, 3)

    def far_pick(block):
        return jnp.stack([block, far_own, far_kind]).astype(jnp.int32)

    def near_pick(block):
        return jnp.stack([block, near_own, near_kind]).astype(jnp.int32)

    def to_near(x):
        return lax.ppermute(x, "row", [(0, 1), (1, 0), (2, 3), (3, 2)])

    def to_far(x):
        return lax.ppermute(x, "row", [(0, 3), (3, 0), (1, 2), (2, 1)])

    gen_message = encode(gen, where, count)
    gen_moved = exchange(gen_message)
    early_part, late_part = ladder_part(gen, ham, *holes, where, after=(gen_message,))
    early = reduced(early_part)
    ham_message = encode(ham, where, count, after=(early_part,))
    (gen_bar,) = bar(read(gen_moved, rows, after=(ham_message,), flops=SLOW), recouple, 1)
    gen_sent = hold(gen_bar, early, LARGE)
    gen_all = lax.all_gather(gen_sent, "row", axis=0, tiled=True)
    ham_moved = exchange(hold(ham_message, gen_sent, 2))
    ham_bar = bar(read(ham_moved, rows), recouple, 2)
    from_far = to_far(ham_bar[0])
    from_near = to_near(ham_bar[1])
    local = local_term(gen_all, ham_bar, *holes)
    send_near = pair_product(far_pick(row ^ 1), gen_all, ham_bar[0], from_far, *holes, after=(local,))
    got_near = to_near(send_near)
    send_far = pair_product(near_pick(3 - row), gen_all, ham_bar[1], from_near, *holes, after=(local,))
    got_far = to_far(send_far)
    sent = (send_near, send_far)
    own = (
        pair_product(far_pick(row), gen_all, ham_bar[0], from_far, *holes, after=sent),
        pair_product(near_pick(row), gen_all, ham_bar[1], from_near, *holes, after=sent),
    )
    message, token = turn(own, (got_near, got_far), local, recouple, count)
    back = exchange(message)
    late = reduced(hold(late_part, token, LARGE))
    return finish(back, early, late, where)[None]


def solution(mesh):
    in_specs = (
        P("chan", "row", None),
        P("chan", "row", None),
        P("chan", None, None),
        P("chan"),
        P("chan", None),
        P("chan", None),
    )
    out_specs = P("chan", "row", None)
    return jax.shard_map(shards, mesh=mesh, in_specs=in_specs, out_specs=out_specs, check_vma=False)
```

time: 411 us -> 263 us (0.64); the launches traced: 404 us -> 262 us
  matrix products: 78.3 us -> 0 us
  waiting for transfers between devices: 135 us -> 59.9 us
  Pallas kernels: 0 us -> 51.6 us
  other arithmetic: 23.3 us -> 0.3 us
  blocking collectives: 115 us -> 104 us
  local copies, waits for them, and re-layouts: 27 us -> 16.4 us
  starting transfers between devices: 11 us -> 16.3 us
    all_gather x4 -> x1, waiting for transfers between devices: 133 us -> 14.9 us  [shards(): gen_all = lax.all_gather(gen_sent, 'row', axis=0, tiled=True)]
    dot_general x7 -> x0, matrix products: 78.3 us -> none  [the longest x6 66.8 us: batched(): jnp.einsum('cij,cjk->cik', left, right, precision=lax.Precision.HIGHEST)]
    pallas_call x0 -> x17, Pallas kernels: none -> 51.6 us  [call(): pl.pallas_call(body, out_shape=out_shape, in_specs=list(in_specs) + [ANY]...]
    all_to_all x1, waiting for transfers between devices: 0.74 us -> 25.7 us  [exchange(): return lax.all_to_all(message, 'chan', 0, 0, tiled=True)]
    all_to_all x3 -> x0, other arithmetic: 21 us -> none  [the longest x1 7.73 us: shards(): lax.all_to_all(ham_live.reshape(piece_shape), 'chan', split_axis=2, conca...]
    ppermute x0 -> x4, waiting for transfers between devices: none -> 19.2 us  [the longest x2 9.95 us: to_near(): return lax.ppermute(x, 'row', [(0, 1), (1, 0), (2, 3), (3, 2)])]
    unnamed x18 -> x34, local copies, waits for them, and re-layouts: 0.04 us -> 16.4 us
    dot_general x2 -> x0, local copies, waits for them, and re-layouts: 11.7 us -> none  [shards(): jnp.einsum('cij,ckj->cik', ph_term, recoupling, precision=lax.Precision.H...]
  transfers between devices with their start and end apart: 5 -> 8, of which waited for: 4 -> 5; matrix products, arithmetic and copies ran while one was open for 22% -> 0% of each run, Pallas kernels for 0% -> 15%
where the time goes in v3:
time: 263 us; the launch traced here: 262 us
  blocking collectives  104 us (40%)
  waiting for transfers between devices  59.9 us (23%)
  Pallas kernels  51.6 us (20%)
  local copies, waits for them, and re-layouts  16.4 us (6%)
  starting transfers between devices  16.3 us (6%)
  between operations  14 us (5%)
    all_to_all x2, blocking collectives, exchange(): return lax.all_to_all(message, 'chan', 0, 0, tiled=True)  104 us
    pallas_call x17, Pallas kernels, call(): pl.pallas_call(body, out_shape=out_shape, in_specs=list(in_specs) + [ANY]...  51.6 us
    all_to_all x1, waiting for transfers between devices, exchange(): return lax.all_to_all(message, 'chan', 0, 0, tiled=True)  25.7 us
    unnamed x34, local copies, waits for them, and re-layouts  16.4 us
    all_gather x1, waiting for transfers between devices, shards(): gen_all = lax.all_gather(gen_sent, 'row', axis=0, tiled=True)  14.9 us
    all_to_all x1, starting transfers between devices, exchange(): return lax.all_to_all(message, 'chan', 0, 0, tiled=True)  12.5 us
    ppermute x2, waiting for transfers between devices, to_near(): return lax.ppermute(x, 'row', [(0, 1), (1, 0), (2, 3), (3, 2)])  9.95 us
    ppermute x2, waiting for transfers between devices, to_far(): return lax.ppermute(x, 'row', [(0, 3), (3, 0), (1, 2), (2, 1)])  9.25 us
  transfers between devices with their start and end apart: 8, of which 5 were waited for; matrix products, arithmetic and copies ran while one was open for 0% of the time, Pallas kernels for 15%

profile of v3, /device:TPU:8, one launch (start us, length us, event | category | flops | bytes accessed | tf_op | source)
XLA Modules:
  0.0 262.1 jit_solution(13212951758358362505)
XLA Ops:
  7.3 1.4 copy-done.7
  8.7 3.0 %shard_map.64.refs_5_ = f32[64,1,6400]{2,1,0:T(1,128)} custom-call(s32[2]{0:T(128)S(1)} %pad_add_fusion.refs_0_, f32[320,1280]{1,0:T(8,128)S(1)} %bitcast.16), custom_call_target="tpu_custom_call" | custom-call | flops 1000 | bytes 4000000 | tf_op jit(solution)/shard_map/pallas_call | solution.py:50
  11.7 12.5 %all-to-all-start = ((f32[64,1,6400]{2,1,0:T(1,128)}), f32[64,1,6400]{2,1,0:T(1,128)}, u32[]{:S(2)}, u32[]{:S(2)}) async-start(f32[64,1,6400]{2,1,0:T(1,128)} %shard_map.64.refs_5_), calls=%async_computation | async-start | bytes 3276800 | tf_op jit(solution)/shard_map/all_to_all | solution.py:400
  24.3 10.3 %shard_map.65 = (f32[1280,512]{1,0:T(8,128)}, f32[1280,768]{1,0:T(8,128)S(1)}) custom-call(s32[2]{0:T(128)S(1)} %pad_add_fusion.refs_0_, f32[320,1280]{1,0:T(8,128)S(1)} %bitcast.17, f32[320,1280]{1,0:T(8,128)S(1)} %bitcast.18, s32[1,1280]{1,0:T(1,128)S(1)} %copy-done.11, s32[1,1280]{1,0:T(1,128)S(1)} %copy-done.12, f32[64,1,6400]{2,1,0:T(1,128)} %shard_map.64.refs_5_), custom_call_target="tpu_custom_call" | custom-call | flops 1000 | bytes 4000000 | tf_op jit(solution)/shard_map/pallas_call | solution.py:50
  34.7 2.0 copy-done.6
  36.9 1.2 copy-done.10
  38.1 1.8 shard_map.66.refs_1_.refs_0_
  39.9 25.7 %all-to-all-done.refs_0_ = f32[64,1,6400]{2,1,0:T(1,128)} async-done(((f32[64,1,6400]{2,1,0:T(1,128)}), f32[64,1,6400]{2,1,0:T(1,128)}, u32[]{:S(2)}, u32[]{:S(2)}) %all-to-all-start) | async-done | bytes 1638432 | tf_op jit(solution)/shard_map/all_to_all | solution.py:400
  65.6 3.9 %shard_map.67 = (bf16[320,1280]{1,0:T(8,128)(2,1)S(1)}, bf16[320,1280]{1,0:T(8,128)(2,1)S(1)}) custom-call(f32[64,1,6400]{2,1,0:T(1,128)} %all-to-all-done.refs_0_, f32[64,1,6400]{2,1,0:T(1,128)S(1)} %shard_map.66.refs_1_.refs_0_), custom_call_target="tpu_custom_call" | custom-call | flops 999999995904 | bytes 4000000 | tf_op jit(solution)/shard_map/pallas_call | solution.py:50
  69.6 2.9 %copy-done.2 = f32[1,1280,1280]{2,1,0:T(8,128)S(1)} copy-done((f32[1,1280,1280]{2,1,0:T(8,128)S(1)}, f32[1,1280,1280]{2,1,0:T(8,128)}, u32[]{:S(2)}) %copy-start.2) | copy-done | bytes 6553624
  72.5 3.4 %shard_map.68.refs_0_ = f32[320,1280]{1,0:T(8,128)S(1)} custom-call(bf16[320,1280]{1,0:T(8,128)(2,1)S(1)} %get-tuple-element.16.refs_0_, bf16[320,1280]{1,0:T(8,128)(2,1)S(1)} %get-tuple-element.17.refs_1_, f32[1280,1280]{1,0:T(8,128)S(1)} %bitcast.11), custom_call_target="tpu_custom_call" | custom-call | flops 1000 | bytes 4000000 | tf_op jit(solution)/shard_map/pallas_call | solution.py:50
  75.9 1.2 copy-done.4
  77.1 1.4 copy-done.5
  78.4 49.2 %all_to_all.15.refs_0_ = f32[64,1,6400]{2,1,0:T(1,128)S(1)} all-to-all(f32[64,1,6400]{2,1,0:T(1,128)S(1)} %shard_map.70), channel_id=1, replica_groups=mesh['chan'=64,'row'=4] {'chan'}, dimensions={0} | all-to-all | bytes 3276800 | tf_op jit(solution)/shard_map/all_to_all | solution.py:400
  127.6 2.5 shard_map.71
  130.1 2.9 %copy-done.3 = f32[1,1280,1280]{2,1,0:T(8,128)S(1)} copy-done((f32[1,1280,1280]{2,1,0:T(8,128)S(1)}, f32[1,1280,1280]{2,1,0:T(8,128)}, u32[]{:S(2)}) %copy-start.3) | copy-done | bytes 6553624
  133.0 3.4 %shard_map.72 = (f32[320,640]{1,0:T(8,128)S(1)}, f32[320,640]{1,0:T(8,128)S(1)}) custom-call(bf16[320,1280]{1,0:T(8,128)(2,1)S(1)} %get-tuple-element.18.refs_0_, bf16[320,1280]{1,0:T(8,128)(2,1)S(1)} %get-tuple-element.19.refs_1_, f32[1280,1280]{1,0:T(8,128)S(1)} %bitcast.12), custom_call_target="tpu_custom_call" | custom-call | flops 1000 | bytes 4000000 | tf_op jit(solution)/shard_map/pallas_call | solution.py:50
  136.4 1.0 collective-permute-start
  138.0 14.9 %all-gather.2.cloned.1.call-done.refs_0_.refs_1_ = f32[1280,1280]{1,0:T(8,128)} async-done(((f32[320,1280]{1,0:T(8,128)}), f32[1280,1280]{1,0:T(8,128)}) %all-gather.2.cloned.1.call-update) | async-done | bytes 6553616 | tf_op jit(solution)/shard_map/all_gather | solution.py:436
  153.0 2.9 %copy-done = f32[1280,1280]{1,0:T(8,128)S(1)} copy-done((f32[1280,1280]{1,0:T(8,128)S(1)}, f32[1280,1280]{1,0:T(8,128)}, u32[]{:S(2)}) %copy-start) | copy-done | bytes 6553624
  155.8 3.5 %shard_map.73.refs_6_.refs_4_ = f32[320,1280]{1,0:T(8,128)S(1)} custom-call(f32[1280,1280]{1,0:T(8,128)S(1)} %copy-done, f32[320,640]{1,0:T(8,128)S(1)} %get-tuple-element.20.refs_1_.refs_2_, f32[320,640]{1,0:T(8,128)S(1)} %get-tuple-element.21.refs_2_, s32[1,1280]{1,0:T(1,128)S(1)} %copy-done.11, s32[1,1280]{1,0:T(1,128)S(1)} %copy-done.12), custom_call_target="tpu_custom_call" | custom-call | flops 1000 | bytes 4000000 | tf_op jit(solution)/shard_map/pallas_call | solution.py:50
  159.3 4.2 %collective-permute-done.refs_3_ = f32[320,640]{1,0:T(8,128)S(1)} collective-permute-done((f32[320,640]{1,0:T(8,128)S(1)}, f32[320,640]{1,0:T(8,128)S(1)}, u32[]{:S(2)}, u32[]{:S(2)}) %collective-permute-start) | collective-permute-done | bytes 819232 | tf_op jit(solution)/shard_map/ppermute | solution.py:427
  163.6 2.5 shard_map.74.refs_6_
  166.1 1.3 collective-permute-start.2
  167.4 2.5 shard_map.75.refs_7_
  170.7 2.5 shard_map.77.refs_1_
  173.2 2.5 shard_map.76.refs_0_
  175.7 9.9 %collective-permute-done.2.refs_2_ = f32[320,640]{1,0:T(8,128)S(1)} collective-permute-done((f32[320,640]{1,0:T(8,128)S(1)}, f32[320,640]{1,0:T(8,128)S(1)}, u32[]{:S(2)}, u32[]{:S(2)}) %collective-permute-start.2) | collective-permute-done | bytes 819232 | tf_op jit(solution)/shard_map/ppermute | solution.py:424
  185.7 5.0 %collective-permute-done.3.refs_3_ = f32[320,640]{1,0:T(8,128)S(1)} collective-permute-done((f32[320,640]{1,0:T(8,128)S(1)}, f32[320,640]{1,0:T(8,128)S(1)}, u32[]{:S(2)}, u32[]{:S(2)}) %collective-permute-start.3) | collective-permute-done | bytes 819232 | tf_op jit(solution)/shard_map/ppermute | solution.py:427
  190.7 4.7 %shard_map.78 = (f32[64,1,6400]{2,1,0:T(1,128)S(1)}, f32[8,128]{1,0:T(8,128)S(1)}) custom-call(f32[320,640]{1,0:T(8,128)S(1)} %shard_map.76.refs_0_, f32[320,640]{1,0:T(8,128)S(1)} %shard_map.77.refs_1_, f32[320,640]{1,0:T(8,128)S(1)} %collective-permute-done.2.refs_2_, f32[320,640]{1,0:T(8,128)S(1)} %collective-permute-done.3.refs_3_, ...), custom_call_target="tpu_custom_call" | custom-call | flops 1000 | bytes 4000000 | tf_op jit(solution)/shard_map/pallas_call | solution.py:50
  196.0 54.5 %all_to_all.16.refs_1_ = f32[64,1,6400]{2,1,0:T(1,128)} all-to-all(f32[64,1,6400]{2,1,0:T(1,128)S(1)} %get-tuple-element.22), channel_id=1, replica_groups=mesh['chan'=64,'row'=4] {'chan'}, dimensions={0} | all-to-all | bytes 3276800 | tf_op jit(solution)/shard_map/all_to_all | solution.py:400
  250.5 5.1 %shard_map.80 = f32[320,1280]{1,0:T(8,128)} custom-call(s32[2]{0:T(128)} %copy-done.13, f32[64,1,6400]{2,1,0:T(1,128)} %all_to_all.16.refs_1_, f32[320,512]{1,0:T(8,128)} %reduce-scatter.3.cloned.1.call-done.refs_1_.refs_2_, f32[320,768]{1,0:T(8,128)} %reduce-scatter.5.cloned.1.call-done.refs_3_), custom_call_target="tpu_custom_call" | custom-call | flops 1000 | bytes 4000000 | tf_op jit(solution)/shard_map/pallas_call | solution.py:50
  (45 shorter events, 2.5 us)
Async XLA Ops:
  7.3 29.6 %copy-start.13 = (s32[2]{0:T(128)}, s32[2]{0:T(128)S(1)}, u32[]{:S(2)}) copy-start(s32[2]{0:T(128)S(1)} %pad_add_fusion.refs_0_) | copy-start | bytes 28
  7.3 1.4 copy-start.7
  8.7 15.6 %copy-start.11 = (s32[1,1280]{1,0:T(1,128)S(1)}, s32[1,1280]{1,0:T(1,128)}, u32[]{:S(2)}) copy-start(s32[1,1280]{1,0:T(1,128)} %refs_4_.11) | copy-start | bytes 15364
  8.7 15.6 %copy-start.12 = (s32[1,1280]{1,0:T(1,128)S(1)}, s32[1,1280]{1,0:T(1,128)}, u32[]{:S(2)}) copy-start(s32[1,1280]{1,0:T(1,128)} %refs_5_.7) | copy-start | bytes 15364
  11.7 12.6 %copy-start.8 = (f32[1,320,1280]{2,1,0:T(8,128)S(1)}, f32[1,320,1280]{2,1,0:T(8,128)}, u32[]{:S(2)}) copy-start(f32[1,320,1280]{2,1,0:T(8,128)} %param.6) | copy-start | bytes 4915204
  11.7 12.6 %copy-start.9 = (f32[1,320,1280]{2,1,0:T(8,128)S(1)}, f32[1,320,1280]{2,1,0:T(8,128)}, u32[]{:S(2)}) copy-start(f32[1,320,1280]{2,1,0:T(8,128)} %param.7) | copy-start | bytes 4915204
  11.7 53.9 %all-to-all-start = ((f32[64,1,6400]{2,1,0:T(1,128)}), f32[64,1,6400]{2,1,0:T(1,128)}, u32[]{:S(2)}, u32[]{:S(2)}) async-start(f32[64,1,6400]{2,1,0:T(1,128)} %shard_map.64.refs_5_), calls=%async_computation | async-start | bytes 3276800 | tf_op jit(solution)/shard_map/all_to_all | solution.py:400
  24.3 52.8 %reduce-scatter.3.cloned.1.call-start = ((), (), s32[]{:S(2)}) async-start(), calls=%async_computation.5 | async-start | bytes 3276800 | tf_op jit(solution)/shard_map/reduce_scatter | solution.py:404
  34.7 2.0 copy-start.6
  36.6 1.4 copy-start.10
  36.7 116.3 %all-gather.2.cloned.1.call-start = ((), (), s32[]{:S(2)}) async-start(), calls=%async_computation.6 | async-start | bytes 8192000 | tf_op jit(solution)/shard_map/all_gather | solution.py:436
  69.6 2.9 %copy-start.2 = (f32[1,1280,1280]{2,1,0:T(8,128)S(1)}, f32[1,1280,1280]{2,1,0:T(8,128)}, u32[]{:S(2)}) copy-start(f32[1,1280,1280]{2,1,0:T(8,128)} %param.8) | copy-start | bytes 19660804
  75.8 1.2 copy-start.4
  77.0 1.4 copy-start.5
  77.0 173.4 %reduce-scatter.5.cloned.1.call-start = ((), (), s32[]{:S(2)}) async-start(), calls=%async_computation.7 | async-start | bytes 4915200 | tf_op jit(solution)/shard_map/reduce_scatter | solution.py:404
  130.1 2.9 %copy-start.3 = (f32[1,1280,1280]{2,1,0:T(8,128)S(1)}, f32[1,1280,1280]{2,1,0:T(8,128)}, u32[]{:S(2)}) copy-start(f32[1,1280,1280]{2,1,0:T(8,128)} %param.8) | copy-start | bytes 19660804
  136.4 27.2 %collective-permute-start = (f32[320,640]{1,0:T(8,128)S(1)}, f32[320,640]{1,0:T(8,128)S(1)}, u32[]{:S(2)}, u32[]{:S(2)}) collective-permute-start(f32[320,640]{1,0:T(8,128)S(1)} %get-tuple-element.20.refs_1_.refs_2_), channel_id=1, source_target_pairs={{0,3},{3,0},{1,2},{2,1},{4,7},{7,4},{5,6},{6,5},{8,11},{11,8},{9,1... | collective-permute-start | bytes 2457608 | tf_op jit(solution)/shard_map/ppermute | solution.py:427
  137.3 30.1 %collective-permute-start.1 = (f32[320,640]{1,0:T(8,128)S(1)}, f32[320,640]{1,0:T(8,128)S(1)}, u32[]{:S(2)}, u32[]{:S(2)}) collective-permute-start(f32[320,640]{1,0:T(8,128)S(1)} %get-tuple-element.21.refs_2_), channel_id=1, source_target_pairs={{0,1},{1,0},{2,3},{3,2},{4,5},{5,4},{6,7},{7,6},{8,9},{9,8},{10,11... | collective-permute-start | bytes 2457608 | tf_op jit(solution)/shard_map/ppermute | solution.py:424
  153.0 2.9 %copy-start = (f32[1280,1280]{1,0:T(8,128)S(1)}, f32[1280,1280]{1,0:T(8,128)}, u32[]{:S(2)}) copy-start(f32[1280,1280]{1,0:T(8,128)} %all-gather.2.cloned.1.call-done.refs_0_.refs_1_) | copy-start | bytes 19660804
  155.8 7.7 %copy-start.1 = (f32[1280,1280]{1,0:T(8,128)S(1)}, f32[1280,1280]{1,0:T(8,128)}, u32[]{:S(2)}) copy-start(f32[1280,1280]{1,0:T(8,128)} %all-gather.2.cloned.1.call-done.refs_0_.refs_1_) | copy-start | bytes 19660804
  166.1 19.6 %collective-permute-start.2 = (f32[320,640]{1,0:T(8,128)S(1)}, f32[320,640]{1,0:T(8,128)S(1)}, u32[]{:S(2)}, u32[]{:S(2)}) collective-permute-start(f32[320,640]{1,0:T(8,128)S(1)} %shard_map.74.refs_6_), channel_id=1, source_target_pairs={{0,1},{1,0},{2,3},{3,2},{4,5},{5,4},{6,7},{7,6},{8,9},{9,8},{10,11... | collective-permute-start | bytes 2457608 | tf_op jit(solution)/shard_map/ppermute | solution.py:424
  169.9 20.8 %collective-permute-start.3 = (f32[320,640]{1,0:T(8,128)S(1)}, f32[320,640]{1,0:T(8,128)S(1)}, u32[]{:S(2)}, u32[]{:S(2)}) collective-permute-start(f32[320,640]{1,0:T(8,128)S(1)} %shard_map.75.refs_7_), channel_id=1, source_target_pairs={{0,3},{3,0},{1,2},{2,1},{4,7},{7,4},{5,6},{6,5},{8,11},{11,8},{9,1... | collective-permute-start | bytes 2457608 | tf_op jit(solution)/shard_map/ppermute | solution.py:427
  170.7 20.0 %slice-start = ((s8[6553600]{0:T(1024)(128)(4,1)}), s8[4194304]{0:T(1024)(128)(4,1)S(1)}, s32[]{:S(2)}) async-start(s8[6553600]{0:T(1024)(128)(4,1)} %bitcast.13), calls=%async_computation.8 | async-start | bytes 8388608
  173.2 17.5 %slice-start.1 = ((s8[6553600]{0:T(1024)(128)(4,1)}), s8[2359296]{0:T(1024)(128)(4,1)S(1)}, s32[]{:S(2)}) async-start(s8[6553600]{0:T(1024)(128)(4,1)} %bitcast.13), calls=%async_computation.9 | async-start | bytes 4718592
  195.4 0.6 copy-start.14
Sparse Core Ops, SparseCore 0:
  36.8 37.5 reduce-scatter.2
  77.2 75.7 all-gather.1
  196.1 48.6 reduce-scatter.4
